TPU v7x, 32 devices: a whole 2x2x4 slice. The times are simulated.
32 devices in a mesh: lon: 8 (over z, y), lat: 4 (over x, core).
Axes of the slice: x: 2, y: 2, z: 4, core: 2. Of those that a mesh axis runs over, the one named last changes fastest.
Arguments:
- ocean_state: float32 [4, 16, 128, 1024], P(None, None, 'lat', 'lon'), may hold values from -4 to 4
- surface_state: float32 [3, 128, 1024], P(None, 'lat', 'lon'), may hold values from -3 to 3
- column_levels: int32 [128, 1024], P('lat', 'lon'), may hold values from 0 to 16
Outputs:
- ocean_next: float32 [4, 16, 128, 1024], P(None, None, 'lat', 'lon')
- surface_next: float32 [3, 128, 1024], P(None, 'lat', 'lon')
Inputs may be any that keep to these rules, and one draw needn't show every extreme that they name: A column holds sea in the levels k < column_levels, counted from the surface; 0 marks land.
All inputs are finite; a program needn't handle non-finite values.
Results may differ from a plain program's by a relative error of at most 0.0003.
Values sent between devices are 32-bit elements; how exact they have to be, the bound alone decides.
A program may use at most 64 MiB of HBM per device.

v0:
```python
import math

import jax
import jax.numpy as jnp
from jax import lax
from jax.sharding import PartitionSpec as P

NSUB = 4


epsilon = 1e-06
tracer_step = 0.1
surface_step = 1.2


def padded_2(block, sides, width):
    for axis, dim in sides:
        count = lax.axis_size(axis)
        forward = [(i, i + 1) for i in range(count - 1)]
        forward.append((count - 1, 0))
        backward = [(target, source) for source, target in forward]
        low = lax.ppermute(
            lax.slice_in_dim(block, block.shape[dim] - width, None, axis=dim), axis, forward
        )
        high = lax.ppermute(lax.slice_in_dim(block, 0, width, axis=dim), axis, backward)
        block = jnp.concatenate([low, block, high], axis=dim)
    return block


def weno_pick(a, b, c, d, e):
    first_poly = (2.0 * a - 7.0 * b + 11.0 * c) / 6.0
    second_poly = (-b + 5.0 * c + 2.0 * d) / 6.0
    third_poly = (2.0 * c + 5.0 * d - e) / 6.0
    first_bend = a - 2.0 * b + c
    first_tilt = a - 4.0 * b + 3.0 * c
    middle_curvature = b - 2.0 * c + d
    second_tilt = b - d
    third_bend = c - 2.0 * d + e
    third_tilt = 3.0 * c - 4.0 * d + e
    first_smooth = epsilon + 13.0 / 12.0 * first_bend * first_bend + 0.25 * first_tilt * first_tilt
    second_smooth = (
        epsilon
        + 13.0 / 12.0 * middle_curvature * middle_curvature
        + 0.25 * second_tilt * second_tilt
    )
    third_smooth = epsilon + 13.0 / 12.0 * third_bend * third_bend + 0.25 * third_tilt * third_tilt
    leading_weight = 0.1 / (first_smooth * first_smooth)
    second_weight = 0.6 / (second_smooth * second_smooth)
    third_weight = 0.3 / (third_smooth * third_smooth)
    total_weight = leading_weight + second_weight + third_weight
    return (
        leading_weight * first_poly + second_weight * second_poly + third_weight * third_poly
    ) / total_weight


def take_slab(source, offset, length, direction):
    return lax.slice_in_dim(source, offset, offset + length, axis=direction)


def flow_divergence(quantity, velocity, wet_mask, cell_count, direction):
    face_count = cell_count + 1
    a = take_slab(quantity, 0, face_count, direction)
    b = take_slab(quantity, 1, face_count, direction)
    c = take_slab(quantity, 2, face_count, direction)
    d = take_slab(quantity, 3, face_count, direction)
    e = take_slab(quantity, 4, face_count, direction)
    far_ahead = take_slab(quantity, 5, face_count, direction)
    left_value = weno_pick(a, b, c, d, e)
    eastern_reconstruction = weno_pick(far_ahead, e, d, c, b)
    face_speed = 0.5 * (
        take_slab(velocity, 2, face_count, direction)
        + take_slab(velocity, 3, face_count, direction)
    )
    face_speed = (
        face_speed
        * take_slab(wet_mask, 2, face_count, direction)
        * take_slab(wet_mask, 3, face_count, direction)
    )
    face_flux = face_speed * jnp.where(face_speed >= 0.0, left_value, eastern_reconstruction)
    return take_slab(face_flux, 1, cell_count, direction) - take_slab(
        face_flux, 0, cell_count, direction
    )


def level_advection(quantities, wet_level):
    row_count = quantities.shape[1] - 6
    col_count = quantities.shape[2] - 6
    along_lon = flow_divergence(
        quantities[:, 3:-3, :], quantities[2:3, 3:-3, :], wet_level[None, 3:-3, :], col_count, 2
    )
    along_lat = flow_divergence(
        quantities[:, :, 3:-3], quantities[3:4, :, 3:-3], wet_level[None, :, 3:-3], row_count, 1
    )
    return along_lon + along_lat


def advect_level(level_pair):
    return level_advection(level_pair[0], level_pair[1])


def layer_step(gathered_arrays, ocean_layer_masks, advection, coriolis):
    levels = gathered_arrays.shape[1]
    thickness = 1.0 / levels
    theta_heat_tracer = gathered_arrays[0]
    haline_tracer = gathered_arrays[1]
    seawater_mass_per_volume = (
        -0.2 * theta_heat_tracer
        + 0.8 * haline_tracer
        - 0.05 * theta_heat_tracer * theta_heat_tracer
        + 0.03 * theta_heat_tracer * haline_tracer
    ) * ocean_layer_masks
    pressure = thickness * (
        jnp.cumsum(seawater_mass_per_volume, axis=0) - 0.5 * seawater_mass_per_volume
    )
    grad_lon = 0.5 * (pressure[:, 3:-3, 4:-2] - pressure[:, 3:-3, 2:-4])
    grad_lat = 0.5 * (pressure[:, 4:-2, 3:-3] - pressure[:, 2:-4, 3:-3])
    interior = gathered_arrays[:, :, 3:-3, 3:-3]
    wet_mask = ocean_layer_masks[:, 3:-3, 3:-3]
    rotation = coriolis[None, :, None]
    accel_u = wet_mask * (-advection[2] + rotation * interior[3] - grad_lon)
    accel_v = wet_mask * (-advection[3] - rotation * interior[2] - grad_lat)
    new_temp = wet_mask * (interior[0] - tracer_step * advection[0])
    new_salt = wet_mask * (interior[1] - tracer_step * advection[1])
    u_star = wet_mask * interior[2] + tracer_step * accel_u
    v_star = wet_mask * interior[3] + tracer_step * accel_v
    depth_rim = thickness * jnp.sum(ocean_layer_masks[:, 1:-1, 1:-1], axis=0)
    safe_depth = jnp.maximum(depth_rim[2:-2, 2:-2], thickness)
    force_lon = thickness * jnp.sum(accel_u, axis=0) / safe_depth
    force_lat = thickness * jnp.sum(accel_v, axis=0) / safe_depth
    return (
        new_temp,
        new_salt,
        u_star,
        v_star,
        force_lon,
        force_lat,
        depth_rim,
        safe_depth,
        wet_mask,
    )


def centered_lon(field):
    padded = jnp.pad(field, ((0, 0), (1, 1)))
    return 0.5 * (padded[:, 2:] - padded[:, :-2])


def centered_lat(field):
    padded = jnp.pad(field, ((1, 1), (0, 0)))
    return 0.5 * (padded[2:, :] - padded[:-2, :])


def substep_update(height, mean_u, mean_v, depth_rim, force_lon, force_lat):
    sea_mask = (depth_rim > 0.0).astype(depth_rim.dtype)
    height = sea_mask * (
        height
        - surface_step * (centered_lon(depth_rim * mean_u) + centered_lat(depth_rim * mean_v))
    )
    mean_u = sea_mask * (mean_u + surface_step * (force_lon - centered_lon(height)))
    mean_v = sea_mask * (mean_v + surface_step * (force_lat - centered_lat(height)))
    return (height, mean_u, mean_v)


def close_rows(padded, folded, rim_width):
    row_total = padded.shape[-2]
    north_tile = lax.axis_index("lat") == lax.axis_size("lat") - 1
    south_tile = lax.axis_index("lat") == 0
    north = jnp.where(north_tile, folded, padded[..., row_total - rim_width :, :])
    south_rows = padded[..., :rim_width, :]
    south = jnp.where(south_tile, jnp.zeros_like(south_rows), south_rows)
    return jnp.concatenate(
        [south, padded[..., rim_width : row_total - rim_width, :], north], axis=-2
    )


def flat_pieces(rows, piece_count):
    entry_count = rows.size
    spare_count = -entry_count % piece_count
    flattened = jnp.concatenate([rows.reshape(-1), jnp.zeros((spare_count,), rows.dtype)])
    return flattened.reshape(piece_count, (entry_count + spare_count) // piece_count)


def whole_rows(domain_pieces, row_shape):
    entry_count = math.prod(row_shape)
    return domain_pieces.reshape(-1)[:entry_count].reshape(row_shape)


def mirror_layer(rows, piece_count):
    pieces = lax.all_to_all(
        flat_pieces(rows, piece_count), "lon", split_axis=0, concat_axis=0, tiled=True
    )
    pieces = lax.all_to_all(
        jnp.flip(pieces, axis=0), "lon", split_axis=0, concat_axis=0, tiled=True
    )
    return whole_rows(pieces, rows.shape)


def mirror_deep(rows, piece_count):
    pieces = lax.all_to_all(
        flat_pieces(rows, piece_count), "lon", split_axis=0, concat_axis=0, tiled=True
    )
    pieces = lax.all_to_all(
        jnp.flip(pieces, axis=0), "lon", split_axis=0, concat_axis=0, tiled=True
    )
    return whole_rows(pieces, rows.shape)


def on_device(ocean_state, surface_state, column_levels):
    levels = ocean_state.shape[1]
    row_count = ocean_state.shape[2]
    col_count = ocean_state.shape[3]
    thickness = 1.0 / levels
    lon_count = lax.axis_size("lon")
    level_index = jnp.arange(levels, dtype=jnp.int32)
    state_planes = ocean_state.reshape(4 * levels, row_count, col_count)
    outgoing = jnp.concatenate([state_planes, column_levels.astype(jnp.float32)[None]], axis=0)
    plane_signs = jnp.concatenate(
        [
            jnp.ones((2 * levels,), jnp.float32),
            -jnp.ones((2 * levels,), jnp.float32),
            jnp.ones((1,), jnp.float32),
        ]
    )
    padded = padded_2(outgoing, (("lon", 2), ("lat", 1)), 3)
    uppermost_lines = mirror_layer(padded[:, row_count : row_count + 3, :], lon_count)
    padded = close_rows(
        padded, jnp.flip(uppermost_lines, axis=(1, 2)) * plane_signs[:, None, None], 3
    )
    gathered_arrays = padded[: 4 * levels].reshape(4, levels, row_count + 6, col_count + 6)
    wet_rim = (level_index.astype(jnp.float32)[:, None, None] < padded[4 * levels][None]).astype(
        jnp.float32
    )
    advection = jnp.moveaxis(
        lax.map(advect_level, (jnp.moveaxis(gathered_arrays, 1, 0), wet_rim)), 0, 1
    )
    first_row = lax.axis_index("lat") * row_count
    latitude = (
        (first_row + jnp.arange(row_count, dtype=jnp.int32)).astype(jnp.float32) + 0.5
    ) / float(lax.axis_size("lat") * row_count)
    coriolis = jnp.sin(math.pi * latitude - 0.5 * math.pi)
    new_temp, new_salt, u_star, v_star, force_lon, force_lat, depth_rim, safe_depth, wet_mask = (
        layer_step(gathered_arrays, wet_rim, advection, coriolis)
    )
    height = surface_state[0]
    mean_u = surface_state[1]
    mean_v = surface_state[2]
    deep_width = 2 * NSUB
    deep_signs = jnp.array([1.0, -1.0, -1.0, 1.0, -1.0, -1.0], jnp.float32)[:, None, None]
    bundle = jnp.stack([height, mean_u, mean_v, depth_rim[2:-2, 2:-2], force_lon, force_lat])
    rim_stack = padded_2(bundle, (("lon", 2), ("lat", 1)), deep_width)
    edge_rows = mirror_deep(rim_stack[:, row_count : row_count + deep_width, :], lon_count)
    rim_stack = close_rows(rim_stack, jnp.flip(edge_rows, axis=(1, 2)) * deep_signs, deep_width)
    height = rim_stack[0]
    mean_u = rim_stack[1]
    mean_v = rim_stack[2]
    for substep in range(NSUB):
        height, mean_u, mean_v = substep_update(
            height, mean_u, mean_v, rim_stack[3], rim_stack[4], rim_stack[5]
        )
    height = height[deep_width:-deep_width, deep_width:-deep_width]
    mean_u = mean_u[deep_width:-deep_width, deep_width:-deep_width]
    mean_v = mean_v[deep_width:-deep_width, deep_width:-deep_width]
    mean_star_u = thickness * jnp.sum(u_star, axis=0) / safe_depth
    mean_star_v = thickness * jnp.sum(v_star, axis=0) / safe_depth
    u_final = wet_mask * (u_star + mean_u - mean_star_u)
    v_final = wet_mask * (v_star + mean_v - mean_star_v)
    return (jnp.stack([new_temp, new_salt, u_final, v_final]), jnp.stack([height, mean_u, mean_v]))


def solution(mesh):
    return jax.shard_map(
        on_device,
        mesh=mesh,
        in_specs=(P(None, None, "lat", "lon"), P(None, "lat", "lon"), P("lat", "lon")),
        out_specs=(P(None, None, "lat", "lon"), P(None, "lat", "lon")),
        check_vma=False,
    )
```

profile of v0, /device:TPU:0, one launch (start us, length us, event | category | flops | bytes accessed | tf_op | source)
XLA Modules:
  0.0 162.3 jit_solution(5548989136297394224)
XLA Ops:
  1.4 1.9 %slice_maximum_fusion = (f32[65,32,3]{2,1,0:T(8,128)S(1)}, f32[65,32,3]{2,1,0:T(8,128)S(1)}) fusion(f32[1,32,128]{2,1,0:T(8,128)S(1)} %convert_bitcast_fusion, f32[64,32,128]{2,1,0:T(8,128)} %bitcast.183), kind=kLoop, calls=%fused_computation.124 | loop fusion | flops 12480 | bytes 1114880 | tf_op jit(solution)/shard_map/concatenate | solution.py:216
  4.0 3.0 %collective-permute-start = (f32[65,32,3]{0,1,2:T(8,128)S(1)}, f32[65,32,3]{0,1,2:T(8,128)S(1)}, u32[]{:S(2)}, u32[]{:S(2)}) collective-permute-start(f32[65,32,3]{0,1,2:T(8,128)S(1)} %copy.17), channel_id=1, source_target_pairs={{0,4},{4,8},{8,12},{12,16},{16,20},{20,24},{24,28},{28,0},{1,5},{5... | collective-permute-start | bytes 74888 | tf_op jit(solution)/shard_map/ppermute | solution.py:22
  7.7 3.1 %collective-permute-start.1 = (f32[65,32,3]{0,1,2:T(8,128)S(1)}, f32[65,32,3]{0,1,2:T(8,128)S(1)}, u32[]{:S(2)}, u32[]{:S(2)}) collective-permute-start(f32[65,32,3]{0,1,2:T(8,128)S(1)} %copy.18), channel_id=1, source_target_pairs={{4,0},{8,4},{12,8},{16,12},{20,16},{24,20},{28,24},{0,28},{5,1},{9... | collective-permute-start | bytes 74888 | tf_op jit(solution)/shard_map/ppermute | solution.py:25
  10.8 1.4 collective-permute-done
  12.2 1.0 copy.19
  13.3 1.1 copy.20
  14.4 1.2 pad_maximum_fusion.11
  15.6 0.9 reshape.65
  16.4 1.5 concatenate.20
  18.0 1.7 %all_to_all.28 = f32[8,1,3267]{2,1,0:T(1,128)} reshape(f32[26136]{0:T(1024)} %concatenate.20) | data formatting | bytes 209088 | tf_op jit(solution)/shard_map/all_to_all | solution.py:189
  19.7 5.6 %all-to-all-start = ((f32[8,1,3267]{2,1,0:T(1,128)}), f32[8,1,3267]{2,1,0:T(1,128)}, u32[]{:S(2)}, u32[]{:S(2)}) async-start(f32[8,1,3267]{2,1,0:T(1,128)} %all_to_all.28), calls=%async_computation | async-start | bytes 212992 | tf_op jit(solution)/shard_map/all_to_all | solution.py:189
  25.4 1.8 %collective-permute-start.3 = (f32[65,3,134]{2,1,0:T(4,128)}, f32[65,3,134]{2,1,0:T(4,128)}, u32[]{:S(2)}, u32[]{:S(2)}) collective-permute-start(f32[65,3,134]{2,1,0:T(4,128)} %get-tuple-element.78), channel_id=1, source_target_pairs={{1,0},{2,1},{3,2},{0,3},{5,4},{6,5},{7,6},{4,7},{9,8},{10,9},{11,1... | collective-permute-start | bytes 313568 | tf_op jit(solution)/shard_map/ppermute | solution.py:25
  27.2 5.4 %all-to-all-done = f32[8,1,3267]{2,1,0:T(1,128)} async-done(((f32[8,1,3267]{2,1,0:T(1,128)}), f32[8,1,3267]{2,1,0:T(1,128)}, u32[]{:S(2)}, u32[]{:S(2)}) %all-to-all-start) | async-done | bytes 104576 | tf_op jit(solution)/shard_map/all_to_all | solution.py:189
  32.6 1.6 copy.55
  34.1 11.5 %rev.16 = f32[8,3267]{1,0:T(8,128)} reverse(f32[8,3267]{1,0:T(8,128)} %bitcast.195), dimensions={0} | reverse | bytes 209088 | tf_op jit(solution)/shard_map/jit(_flip)/rev | solution.py:193
  45.6 1.7 %copy.21 = f32[8,1,3267]{2,1,0:T(1,128)} copy(f32[8,1,3267]{2,0,1:T(8,128)} %bitcast.196) | data formatting | bytes 209088 | tf_op jit(solution)/shard_map/all_to_all | solution.py:192
  47.3 4.1 %all-to-all-start.1 = ((f32[8,1,3267]{2,1,0:T(1,128)}), f32[8,1,3267]{2,1,0:T(1,128)}, u32[]{:S(2)}, u32[]{:S(2)}) async-start(f32[8,1,3267]{2,1,0:T(1,128)} %copy.21), calls=%async_computation.1 | async-start | bytes 212992 | tf_op jit(solution)/shard_map/all_to_all | solution.py:192
  51.5 7.1 %all-to-all-done.1 = f32[8,1,3267]{2,1,0:T(1,128)} async-done(((f32[8,1,3267]{2,1,0:T(1,128)}), f32[8,1,3267]{2,1,0:T(1,128)}, u32[]{:S(2)}, u32[]{:S(2)}) %all-to-all-start.1) | async-done | bytes 104576 | tf_op jit(solution)/shard_map/all_to_all | solution.py:192
  58.6 1.8 %reduce = f32[8,3267]{1,0:T(8,128)} reduce(f32[8,1,3267]{2,1,0:T(1,128)} %all-to-all-done.1, f32[]{:T(128)} %constant.176), dimensions={1}, to_apply=%all_to_all.32.reduce_sub_computation | reduce | bytes 209092 | tf_op jit(solution)/shard_map/all_to_all | solution.py:192
  60.4 1.6 %reshape.66 = f32[26136]{0:T(1024)} reshape(f32[8,3267]{1,0:T(8,128)} %reduce) | data formatting | bytes 209088 | tf_op jit(solution)/shard_map/reshape | solution.py:185
  62.0 1.9 %reshape.67 = f32[65,3,134]{2,1,0:T(4,128)} reshape(f32[26130]{0:T(1024)} %bitcast.197) | data formatting | bytes 209040 | tf_op jit(solution)/shard_map/reshape | solution.py:185
  63.9 2.1 %reverse = f32[65,3,256]{2,1,0:T(4,128)} reverse(f32[65,3,256]{2,1,0:T(4,128)} %bitcast.193), dimensions={1,2} | reverse | bytes 399360
  66.0 1.3 multiply_select_fusion
  67.6 2.1 %fusion.73 = f32[16,38,134]{2,1,0:T(8,128)} fusion(f32[65,3,134]{2,1,0:T(4,128)S(1)} %multiply_select_fusion, f32[65,32,3]{2,1,0:T(8,128)S(1)} %copy.20, f32[1,32,128]{2,1,0:T(8,128)S(1)} %convert_bitcast_fusion, f32[64,32,128]{2,1,0:T(8,128)S(1)} %bitcast.186, f32[65,32,3]{2,1,0:T(8,128)S(1)} %copy.19, f32[65,3,134]{2,1,0:T(4,128)S(1)} %broadcast_select_fusion, ...), kind=kOutput, calls=%fused_computation.122 | output fusion | flops 4888320 | bytes 1670240 | tf_op jit(solution)/shard_map/jit(cumsum)/reduce_window_sum | solution.py:113
  69.6 1.2 pad_maximum_fusion
  70.8 0.9 slice_reduce_fusion
  71.8 0.9 copy-done.2
  72.8 34.9 %while.10 = (s32[]{:T(128)}, f32[16,4,32,128]{3,2,0,1:T(8,128)}, f32[16,4,38,134]{3,2,0,1:T(8,128)S(1)}, f32[16,38,134]{2,1,0:T(8,128)S(1)}, s32[]{:T(128)}, /*index=5*/s32[]{:T(128)}, s32[]{}, s32[]{}) while((s32[]{:T(128)}, f32[16,4,32,128]{3,2,0,1:T(8,128)}, f32[16,4,38,134]{3,2,0,1:T(8,128)S(1)}, f32[16,38,134]{2,1,0:T(8,128)S(1)}, ...), condition=%wide.region_1.2_spmd, body=%wide.region_0.1_spmd.sunk | while | flops 4300324 | bytes 1722989 | solution.py:234
  107.7 3.9 %fusion.167 = (f32[32,128]{1,0:T(8,128)S(1)}, f32[32,128]{1,0:T(8,128)S(1)}, f32[32,128]{1,0:T(8,128)S(1)}, f32[32,128]{1,0:T(8,128)S(1)}, f32[16,32,128]{2,1,0:...) fusion(f32[4,16,38,134]{3,2,1,0:T(8,128)S(1)} %bitcast.189, ...), kind=kLoop, calls=%fused_computation.299 | loop fusion | flops 1949696 | bytes 4522112 | tf_op jit(solution)/shard_map/reduce_sum | solution.py:263
  111.6 1.5 multiply_divide_fusion.1
  113.5 4.4 %collective-permute-start.5 = (f32[6,32,8]{2,1,0:T(8,128)S(1)}, f32[6,32,8]{2,1,0:T(8,128)S(1)}, u32[]{:S(2)}, u32[]{:S(2)}) collective-permute-start(f32[6,32,8]{2,1,0:T(8,128)S(1)} %get-tuple-element.94), channel_id=1, source_target_pairs={{4,0},{8,4},{12,8},{16,12},{20,16},{24,20},{28,24},{0,28},{5,1},{9... | collective-permute-start | bytes 18440 | tf_op jit(solution)/shard_map/ppermute | solution.py:25
  117.9 2.6 %collective-permute-done.4 = f32[6,32,8]{2,1,0:T(8,128)S(1)} collective-permute-done((f32[6,32,8]{2,1,0:T(8,128)S(1)}, f32[6,32,8]{2,1,0:T(8,128)S(1)}, u32[]{:S(2)}, u32[]{:S(2)}) %collective-permute-start.4) | collective-permute-done | bytes 6176 | tf_op jit(solution)/shard_map/ppermute | solution.py:22
  120.5 0.8 pad_maximum_fusion.18
  121.3 1.5 all_to_all.33
  122.8 6.0 %all-to-all-start.2 = ((f32[8,1,864]{2,1,0:T(1,128)}), f32[8,1,864]{2,1,0:T(1,128)}, u32[]{:S(2)}, u32[]{:S(2)}) async-start(f32[8,1,864]{2,1,0:T(1,128)} %all_to_all.33), calls=%async_computation.2 | async-start | bytes 57344 | tf_op jit(solution)/shard_map/all_to_all | solution.py:199
  128.8 1.7 %collective-permute-start.7 = (f32[6,8,144]{2,1,0:T(8,128)}, f32[6,8,144]{2,1,0:T(8,128)}, u32[]{:S(2)}, u32[]{:S(2)}) collective-permute-start(f32[6,8,144]{2,1,0:T(8,128)} %get-tuple-element.92), channel_id=1, source_target_pairs={{1,0},{2,1},{3,2},{0,3},{5,4},{6,5},{7,6},{4,7},{9,8},{10,9},{11,1... | collective-permute-start | bytes 82952 | tf_op jit(solution)/shard_map/ppermute | solution.py:25
  130.6 5.0 %all-to-all-done.2 = f32[8,1,864]{2,1,0:T(1,128)} async-done(((f32[8,1,864]{2,1,0:T(1,128)}), f32[8,1,864]{2,1,0:T(1,128)}, u32[]{:S(2)}, u32[]{:S(2)}) %all-to-all-start.2) | async-done | bytes 27680 | tf_op jit(solution)/shard_map/all_to_all | solution.py:199
  135.6 1.4 copy.56
  136.9 3.8 %rev.18 = f32[8,864]{1,0:T(8,128)} reverse(f32[8,864]{1,0:T(8,128)} %bitcast.201), dimensions={0} | reverse | bytes 55296 | tf_op jit(solution)/shard_map/jit(_flip)/rev | solution.py:203
  140.8 1.4 copy.24
  142.1 3.9 %all-to-all-start.3 = ((f32[8,1,864]{2,1,0:T(1,128)}), f32[8,1,864]{2,1,0:T(1,128)}, u32[]{:S(2)}, u32[]{:S(2)}) async-start(f32[8,1,864]{2,1,0:T(1,128)} %copy.24), calls=%async_computation.3 | async-start | bytes 57344 | tf_op jit(solution)/shard_map/all_to_all | solution.py:202
  146.7 6.0 %all-to-all-done.3 = f32[8,1,864]{2,1,0:T(1,128)} async-done(((f32[8,1,864]{2,1,0:T(1,128)}), f32[8,1,864]{2,1,0:T(1,128)}, u32[]{:S(2)}, u32[]{:S(2)}) %all-to-all-start.3) | async-done | bytes 27680 | tf_op jit(solution)/shard_map/all_to_all | solution.py:202
  152.8 1.4 reduce.1
  154.2 1.5 reshape_reshape.4
  155.6 1.5 reverse.1
  157.1 0.9 multiply_select_fusion.1
  158.1 1.2 pad_maximum_fusion.7
  161.3 1.0 pad_maximum_fusion.2
  (191 shorter events, 40.2 us)
Async XLA Ops:
  4.0 8.2 %collective-permute-start = (f32[65,32,3]{0,1,2:T(8,128)S(1)}, f32[65,32,3]{0,1,2:T(8,128)S(1)}, u32[]{:S(2)}, u32[]{:S(2)}) collective-permute-start(f32[65,32,3]{0,1,2:T(8,128)S(1)} %copy.17), channel_id=1, source_target_pairs={{0,4},{4,8},{8,12},{12,16},{16,20},{20,24},{24,28},{28,0},{1,5},{5... | collective-permute-start | bytes 74888 | tf_op jit(solution)/shard_map/ppermute | solution.py:22
  7.7 5.6 %collective-permute-start.1 = (f32[65,32,3]{0,1,2:T(8,128)S(1)}, f32[65,32,3]{0,1,2:T(8,128)S(1)}, u32[]{:S(2)}, u32[]{:S(2)}) collective-permute-start(f32[65,32,3]{0,1,2:T(8,128)S(1)} %copy.18), channel_id=1, source_target_pairs={{4,0},{8,4},{12,8},{16,12},{20,16},{24,20},{28,24},{0,28},{5,1},{9... | collective-permute-start | bytes 74888 | tf_op jit(solution)/shard_map/ppermute | solution.py:25
  10.8 3.6 %copy-start = (f32[4,16,32,128]{3,2,1,0:T(8,128)S(1)}, f32[4,16,32,128]{3,2,1,0:T(8,128)}, u32[]{:S(2)}) copy-start(f32[4,16,32,128]{3,2,1,0:T(8,128)} %param.6) | copy-start | bytes 3145732
  19.7 12.9 %all-to-all-start = ((f32[8,1,3267]{2,1,0:T(1,128)}), f32[8,1,3267]{2,1,0:T(1,128)}, u32[]{:S(2)}, u32[]{:S(2)}) async-start(f32[8,1,3267]{2,1,0:T(1,128)} %all_to_all.28), calls=%async_computation | async-start | bytes 212992 | tf_op jit(solution)/shard_map/all_to_all | solution.py:189
  25.3 26.1 %collective-permute-start.2 = (f32[65,3,134]{2,1,0:T(4,128)S(1)}, f32[65,3,134]{2,1,0:T(4,128)}, u32[]{:S(2)}, u32[]{:S(2)}) collective-permute-start(f32[65,3,134]{2,1,0:T(4,128)S(1)} %get-tuple-element.77), channel_id=1, source_target_pairs={{0,1},{1,2},{2,3},{3,0},{4,5},{5,6},{6,7},{7,4},{8,9},{9,10},{10,1... | collective-permute-start | bytes 313568 | tf_op jit(solution)/shard_map/ppermute | solution.py:22
  25.4 40.6 %collective-permute-start.3 = (f32[65,3,134]{2,1,0:T(4,128)}, f32[65,3,134]{2,1,0:T(4,128)}, u32[]{:S(2)}, u32[]{:S(2)}) collective-permute-start(f32[65,3,134]{2,1,0:T(4,128)} %get-tuple-element.78), channel_id=1, source_target_pairs={{1,0},{2,1},{3,2},{0,3},{5,4},{6,5},{7,6},{4,7},{9,8},{10,9},{11,1... | collective-permute-start | bytes 313568 | tf_op jit(solution)/shard_map/ppermute | solution.py:25
  47.3 18.8 %copy-start.13 = (f32[65]{0:T(128)S(1)}, f32[65]{0:T(128)}, u32[]{:S(2)}) copy-start(f32[65]{0:T(128)} %constant.97.clone.1) | copy-start | bytes 784
  47.3 11.3 %all-to-all-start.1 = ((f32[8,1,3267]{2,1,0:T(1,128)}), f32[8,1,3267]{2,1,0:T(1,128)}, u32[]{:S(2)}, u32[]{:S(2)}) async-start(f32[8,1,3267]{2,1,0:T(1,128)} %copy.21), calls=%async_computation.1 | async-start | bytes 212992 | tf_op jit(solution)/shard_map/all_to_all | solution.py:192
  67.5 3.2 %copy-start.1 = (f32[16,38,134]{2,1,0:T(8,128)}, f32[16,38,134]{2,1,0:T(8,128)S(1)}, u32[]{:S(2)}) copy-start(f32[16,38,134]{2,1,0:T(8,128)S(1)} %compare_convert_fusion) | copy-start | bytes 977668
  71.7 1.1 copy-start.2
  107.7 5.4 %copy-start.6 = (f32[3,32,128]{2,1,0:T(8,128)S(1)}, f32[3,32,128]{2,1,0:T(8,128)}, u32[]{:S(2)}) copy-start(f32[3,32,128]{2,1,0:T(8,128)} %param.7) | copy-start | bytes 147460
  113.1 8.2 %copy-start.9 = (f32[1,32,128]{2,1,0:T(8,128)}, f32[1,32,128]{2,1,0:T(8,128)S(1)}, u32[]{:S(2)}) copy-start(f32[1,32,128]{2,1,0:T(8,128)S(1)} %get-tuple-element.102) | copy-start | bytes 49156
  113.1 8.2 %copy-start.10 = (f32[1,32,128]{2,1,0:T(8,128)}, f32[1,32,128]{2,1,0:T(8,128)S(1)}, u32[]{:S(2)}) copy-start(f32[1,32,128]{2,1,0:T(8,128)S(1)} %get-tuple-element.103) | copy-start | bytes 49156
  113.2 7.4 %collective-permute-start.4 = (f32[6,32,8]{2,1,0:T(8,128)S(1)}, f32[6,32,8]{2,1,0:T(8,128)S(1)}, u32[]{:S(2)}, u32[]{:S(2)}) collective-permute-start(f32[6,32,8]{2,1,0:T(8,128)S(1)} %get-tuple-element.93), channel_id=1, source_target_pairs={{0,4},{4,8},{8,12},{12,16},{16,20},{20,24},{24,28},{28,0},{1,5},{5... | collective-permute-start | bytes 18440 | tf_op jit(solution)/shard_map/ppermute | solution.py:22
  113.5 7.0 %collective-permute-start.5 = (f32[6,32,8]{2,1,0:T(8,128)S(1)}, f32[6,32,8]{2,1,0:T(8,128)S(1)}, u32[]{:S(2)}, u32[]{:S(2)}) collective-permute-start(f32[6,32,8]{2,1,0:T(8,128)S(1)} %get-tuple-element.94), channel_id=1, source_target_pairs={{4,0},{8,4},{12,8},{16,12},{20,16},{24,20},{28,24},{0,28},{5,1},{9... | collective-permute-start | bytes 18440 | tf_op jit(solution)/shard_map/ppermute | solution.py:25
  120.5 0.8 copy-start.7
  120.5 0.8 copy-start.8
  122.8 12.8 %all-to-all-start.2 = ((f32[8,1,864]{2,1,0:T(1,128)}), f32[8,1,864]{2,1,0:T(1,128)}, u32[]{:S(2)}, u32[]{:S(2)}) async-start(f32[8,1,864]{2,1,0:T(1,128)} %all_to_all.33), calls=%async_computation.2 | async-start | bytes 57344 | tf_op jit(solution)/shard_map/all_to_all | solution.py:199
  128.8 17.3 %collective-permute-start.6 = (f32[6,8,144]{2,1,0:T(8,128)}, f32[6,8,144]{2,1,0:T(8,128)}, u32[]{:S(2)}, u32[]{:S(2)}) collective-permute-start(f32[6,8,144]{2,1,0:T(8,128)} %get-tuple-element.91), channel_id=1, source_target_pairs={{0,1},{1,2},{2,3},{3,0},{4,5},{5,6},{6,7},{7,4},{8,9},{9,10},{10,1... | collective-permute-start | bytes 82952 | tf_op jit(solution)/shard_map/ppermute | solution.py:22
  128.8 28.3 %collective-permute-start.7 = (f32[6,8,144]{2,1,0:T(8,128)}, f32[6,8,144]{2,1,0:T(8,128)}, u32[]{:S(2)}, u32[]{:S(2)}) collective-permute-start(f32[6,8,144]{2,1,0:T(8,128)} %get-tuple-element.92), channel_id=1, source_target_pairs={{1,0},{2,1},{3,2},{0,3},{5,4},{6,5},{7,6},{4,7},{9,8},{10,9},{11,1... | collective-permute-start | bytes 82952 | tf_op jit(solution)/shard_map/ppermute | solution.py:25
  142.1 10.6 %all-to-all-start.3 = ((f32[8,1,864]{2,1,0:T(1,128)}), f32[8,1,864]{2,1,0:T(1,128)}, u32[]{:S(2)}, u32[]{:S(2)}) async-start(f32[8,1,864]{2,1,0:T(1,128)} %copy.24), calls=%async_computation.3 | async-start | bytes 57344 | tf_op jit(solution)/shard_map/all_to_all | solution.py:202
  159.5 1.5 copy-start.4
  159.5 1.5 copy-start.5
  159.5 1.5 copy-start.11
  159.5 1.5 copy-start.12
  160.2 1.1 copy-start.3
where the time goes:
time: 165 us; the launch traced here: 162 us
  other arithmetic  57.4 us (35%)
  local copies, waits for them, and re-layouts  41.9 us (25%)
  starting transfers between devices  34 us (21%)
  waiting for transfers between devices  27.6 us (17%)
    mul x32, other arithmetic, flow_divergence(): face_speed * jnp.where(face_speed >= 0.0, left_value, eastern_reconstruct...  18.3 us
    dynamic_update_slice x16, other arithmetic, on_device(): lax.map(advect_level, (jnp.moveaxis(gathered_arrays, 1, 0), wet_rim))  11.6 us
    rev x1, local copies, waits for them, and re-layouts, mirror_layer(): jnp.flip(pieces, axis=0)  11.5 us
    ppermute x4, starting transfers between devices, padded_2(): lax.ppermute(lax.slice_in_dim(block, 0, width, axis=dim), axis, backward)  11 us
    unnamed x32, local copies, waits for them, and re-layouts  7.47 us
    all_to_all x1, waiting for transfers between devices, mirror_layer(): lax.all_to_all(jnp.flip(pieces, axis=0), 'lon', split_axis=0, concat_axis...  7.11 us
    all_to_all x1, waiting for transfers between devices, mirror_deep(): lax.all_to_all(jnp.flip(pieces, axis=0), 'lon', split_axis=0, concat_axis...  6.03 us
    all_to_all x1, starting transfers between devices, mirror_deep(): lax.all_to_all(flat_pieces(rows, piece_count), 'lon', split_axis=0, conca...  5.99 us
  transfers between devices with their start and end apart: 12, of which 6 were waited for; matrix products, arithmetic and copies ran while one was open for 22% of the time, Pallas kernels for 0%

commit v1 on v0

v1 whole, which is shorter than its diff:
```python
import functools
import math

import jax
import jax.numpy as jnp
from jax import lax
from jax.experimental import pallas as pl
from jax.experimental.pallas import tpu as pltpu
from jax.sharding import PartitionSpec as P

NSUB = 4
DEEP = 2 * NSUB
SUB = 8
epsilon = 1e-06
tracer_step = 0.1
surface_step = 1.2
f32 = jnp.float32


def face_flux(s, q0, q1, dm2, dm1, d0, dp1, dp2):
    pos = s >= 0.0
    c = jnp.where(pos, q0, q1)
    d1 = jnp.where(pos, dm2, dp2)
    d2 = jnp.where(pos, dm1, dp1)
    d3 = d0
    d4 = jnp.where(pos, dp1, dm1)
    k = 13.0 / 3.0
    b1 = d2 - d1
    b2 = d3 - d2
    b3 = d4 - d3
    t1 = 3.0 * d2 - d1
    t2 = d2 + d3
    t3 = d4 - 3.0 * d3
    s1 = (k * b1) * b1 + t1 * t1 + 4.0 * epsilon
    s2 = (k * b2) * b2 + t2 * t2 + 4.0 * epsilon
    s3 = (k * b3) * b3 + t3 * t3 + 4.0 * epsilon
    p23 = s2 * s3
    p13 = s1 * s3
    p12 = s1 * s2
    w1 = p23 * p23
    w2 = 6.0 * (p13 * p13)
    w3 = 3.0 * (p12 * p12)
    top = w1 * (2.0 * t1 - d2) + w2 * (t2 + d3) + w3 * (d3 - t3)
    total = 6.0 * (w1 + w2 + w3)
    r = pl.reciprocal(total, approx=True)
    r = r * (2.0 - total * r)
    return s * c + jnp.abs(s) * (top * r)


def left(x, n):
    return pltpu.roll(x, x.shape[-1] - n, axis=x.ndim - 1)


def right(x, n):
    return pltpu.roll(x, n, axis=x.ndim - 1)


def kernel(nx, ny, ocean, surface, levels_in, out, surf_out, ext, lon_own, lon_in, lat_out, lat_in, sa, sf,
           sa_lon, sf_lon, sa_north, sf_north, extra_lon, extra_lat, speed_lon, speed_lat, pbuf, fbuf,
           local_sem, send_sem, recv_sem):
    nlev, rows, cols = ocean.shape[1], ocean.shape[2], ocean.shape[3]
    top = SUB + rows
    full = top + SUB
    thickness = 1.0 / nlev
    wide = 8
    x = lax.axis_index("lon")
    y = lax.axis_index("lat")
    at_north = y == ny - 1
    east = {"lon": lax.rem(x + 1, nx), "lat": y}
    west = {"lon": lax.rem(x + nx - 1, nx), "lat": y}
    north = {"lon": jnp.where(at_north, nx - 1 - x, x), "lat": jnp.where(at_north, y, y + 1)}
    south = {"lon": x, "lat": jnp.maximum(y - 1, 0)}
    fold = jnp.where(at_north, 1, 0)
    far_row = pl.multiple_of(fold * top, SUB)

    load = pltpu.make_async_copy(ocean, ext.at[:, :, SUB:top, :], local_sem)
    load.start()

    sa[0:3, 0, SUB:top, :] = surface[...]
    sa[3, 0, SUB:top, :] = levels_in[...].astype(f32)

    @pl.when(y == 0)
    def _():
        sa[:, :, 0:SUB, :] = jnp.zeros((4, 2, SUB, cols), f32)
        sf[:, :, 0:SUB, :] = jnp.zeros((2, 2, SUB, cols), f32)
        lat_in[0] = jnp.zeros(lat_in.shape[1:], f32)

    barrier = pltpu.get_barrier_semaphore()
    for target in (east, west, north):
        pl.semaphore_signal(barrier, inc=1, device_id=target, device_id_type=pl.DeviceIdType.MESH)

    @pl.when(y > 0)
    def _():
        pl.semaphore_signal(barrier, inc=1, device_id=south, device_id_type=pl.DeviceIdType.MESH)

    pl.semaphore_wait(barrier, 3 + jnp.where(y > 0, 1, 0))

    def remote(src, dst, send, recv, target):
        return pltpu.make_async_remote_copy(
            src_ref=src, dst_ref=dst, send_sem=send_sem.at[send], recv_sem=recv_sem.at[recv],
            device_id=target, device_id_type=pl.DeviceIdType.MESH)

    class LonPair:
        def __init__(self, src, dst, base):
            self.go_east = remote(src, dst.at[0], base, base, east)
            self.go_west = remote(src, dst.at[1], base + 1, base + 1, west)

        def start(self):
            self.go_east.start()
            self.go_west.start()

        def wait_recv(self):
            self.go_east.wait_recv()
            self.go_west.wait_recv()

        def wait_send(self):
            self.go_east.wait_send()
            self.go_west.wait_send()

    class LatPair:
        def __init__(self, north_src, north_dst, south_src, dst_south, dst_north, base):
            self.go_north = remote(north_src, north_dst, base, base + fold, north)
            self.go_south = remote(south_src, dst_north, base + 1, base + 1, south)
            self.from_south = remote(north_src, dst_south, base, base, south)

        def start(self):
            self.go_north.start()

            @pl.when(y > 0)
            def _():
                self.go_south.start()

        def wait_recv(self):
            self.go_south.wait_recv()

            @pl.when(y > 0)
            def _():
                self.from_south.wait_recv()

        def wait_send(self):
            self.go_north.wait_send()

            @pl.when(y > 0)
            def _():
                self.go_south.wait_send()

    surf_lon = LonPair(sa.at[:, 0, SUB:top, :], sa_lon, 0)
    level_lon = LonPair(lon_own, lon_in, 2)
    force_lon_pair = LonPair(sf.at[:, 0, SUB:top, :], sf_lon, 4)
    level_lat = LatPair(lat_out.at[0], lat_in.at[fold], lat_out.at[1], lat_in.at[0], lat_in.at[1], 6)
    surf_lat = LatPair(sa_north, sa.at[:, :, pl.ds(far_row, SUB), :], sa.at[:, :, SUB:2 * SUB, :],
                       sa.at[:, :, 0:SUB, :], sa.at[:, :, top:full, :], 8)
    force_lat_pair = LatPair(sf_north, sf.at[:, :, pl.ds(far_row, SUB), :], sf.at[:, :, SUB:2 * SUB, :],
                             sf.at[:, :, 0:SUB, :], sf.at[:, :, top:full, :], 10)

    surf_lon.start()

    lane = lax.broadcasted_iota(jnp.int32, (rows, cols), 1)
    lane_full = lax.broadcasted_iota(jnp.int32, (full, cols), 1)
    spot = lane % wide
    owner = lane // wide
    sub8 = lax.broadcasted_iota(jnp.int32, (SUB, cols), 0)

    def mirrored(block):
        count = block.shape[0]
        a = lax.broadcasted_iota(jnp.int32, (cols, cols), 0)
        b = lax.broadcasted_iota(jnp.int32, (cols, cols), 1)
        flip_cols = (a + b == cols - 1).astype(f32)
        a = lax.broadcasted_iota(jnp.int32, (count, count), 0)
        b = lax.broadcasted_iota(jnp.int32, (count, count), 1)
        flip_rows = ((a // SUB == b // SUB) & (a % SUB + b % SUB == SUB - 1)).astype(f32)
        block = lax.dot(block, flip_cols, precision=lax.Precision.HIGHEST, preferred_element_type=f32)
        return lax.dot(flip_rows, block, precision=lax.Precision.HIGHEST, preferred_element_type=f32)

    load.wait()

    for q in range(4):
        pack = jnp.zeros((rows, cols), f32)
        for k in range(nlev):
            pack = jnp.where(owner == k, right(ext[q, k, SUB:top, :], wide * k + 3), pack)
        lon_own[q] = pack
    level_lon.start()

    half = nlev // 2
    for q in range(4):
        for h in range(half):
            n0 = ext[q, 2 * h, top - SUB:top, :]
            n1 = ext[q, 2 * h + 1, top - SUB:top, :]
            lat_out[0, q * half + h] = jnp.where(sub8 >= 4, n0, pltpu.roll(n1, 4, axis=0))
            s0 = ext[q, 2 * h, SUB:2 * SUB, :]
            s1 = ext[q, 2 * h + 1, SUB:2 * SUB, :]
            lat_out[1, q * half + h] = jnp.where(sub8 < 4, s0, pltpu.roll(s1, 4, axis=0))

    @pl.when(at_north)
    def _():
        for q in range(4):
            sign = 1.0 if q < 2 else -1.0
            block = lat_out[0, q * half:(q + 1) * half].reshape(half * SUB, cols)
            lat_out[0, q * half:(q + 1) * half] = (sign * mirrored(block)).reshape(half, SUB, cols)

    level_lat.start()

    def close_lon(fields, arrived, count):
        for f in range(count):
            fields[f, 1, SUB:top, :] = jnp.where(lane < cols // 2, arrived[1, f], arrived[0, f])

    def stage_north(fields, staged, signs):
        count = len(signs)
        for f in range(count):
            for part in range(2):
                staged[f, part] = fields[f, part, top - SUB:top, :]

        @pl.when(at_north)
        def _():
            for f in range(count):
                block = staged[f].reshape(2 * SUB, cols)
                staged[f] = (signs[f] * mirrored(block)).reshape(2, SUB, cols)

    surf_lon.wait_recv()
    close_lon(sa, sa_lon, 4)
    stage_north(sa, sa_north, (1.0, -1.0, -1.0, 1.0))
    surf_lat.start()

    level_lon.wait_recv()
    level_lat.wait_recv()
    surf_lat.wait_recv()

    for q in range(4):
        for h in range(half):
            for side, place in ((0, 0), (1, top)):
                block = lat_in[side, q * half + h]
                ext[q, 2 * h, place:place + SUB, :] = block
                ext[q, 2 * h + 1, place:place + SUB, :] = pltpu.roll(block, 4, axis=0)

    def lon_pack(q):
        return jnp.where(spot < 3, lon_in[0, q], lon_own[q])

    count_here = sa[3, 0, SUB:top, :]
    count_beside = sa[3, 1, SUB:top, :]
    level_of = owner.astype(f32)
    edge_wet = ((count_beside[:, cols - 1:cols] > level_of) & (count_here[:, 0:1] > level_of)).astype(f32)
    pack_u = lon_pack(2)
    edge_speed = 0.5 * (pack_u + left(pack_u, 1)) * edge_wet
    for q in range(4):
        pack = lon_pack(q)
        d = left(pack, 1) - pack
        extra_lon[q] = face_flux(edge_speed, pack, left(pack, 1), right(d, 2), right(d, 1), d, left(d, 1),
                                 left(d, 2))

    level_row = lax.broadcasted_iota(jnp.int32, (nlev, cols), 0).astype(f32)
    row_wet = ((sa[3, 0, SUB - 1:SUB, :] > level_row) & (sa[3, 0, SUB:SUB + 1, :] > level_row)).astype(f32)
    row_speed = 0.5 * (ext[3, :, SUB - 1, :] + ext[3, :, SUB, :]) * row_wet
    for q in range(4):
        cell = [ext[q, :, SUB - 3 + i, :] for i in range(6)]
        d = [cell[i + 1] - cell[i] for i in range(5)]
        extra_lat[q] = face_flux(row_speed, cell[2], cell[3], *d)

    def beside(q, k):
        both = jnp.where(spot < 3, lon_in[0, q], lon_in[1, q])
        return pltpu.roll(both, cols - 3 - wide * k, axis=1)

    def following(c, h):
        return left(jnp.where(lane == 0, h, c), 1)

    def advect(q, k, s_lon, s_lat):
        c = ext[q, k, SUB:top, :]
        h = beside(q, k)
        c1 = following(c, h)
        d = c1 - c
        dh = following(h, c) - h
        flux = face_flux(
            s_lon, c, c1,
            right(jnp.where(lane >= cols - 2, dh, d), 2),
            right(jnp.where(lane >= cols - 1, dh, d), 1),
            d,
            left(jnp.where(lane < 1, dh, d), 1),
            left(jnp.where(lane < 2, dh, d), 2))
        edge = pltpu.roll(extra_lon[q], cols - 2 - wide * k, axis=1)
        along = flux - jnp.where(lane == 0, edge, right(flux, 1))
        cell = [ext[q, k, SUB - 2 + i:top - 2 + i, :] for i in range(6)]
        d = [cell[i + 1] - cell[i] for i in range(5)]
        flux = face_flux(s_lat, cell[2], cell[3], *d)
        fbuf[SUB:top, :] = flux
        fbuf[SUB - 1:SUB, :] = extra_lat[q, pl.ds(k, 1), :]
        return along + (flux - fbuf[SUB - 1:top - 1, :])

    row = lax.broadcasted_iota(jnp.int32, (rows, cols), 0)
    latitude = ((y * rows + row).astype(f32) + 0.5) / float(ny * rows)
    coriolis = jnp.sin(math.pi * latitude - 0.5 * math.pi)

    def density(t, s, wet):
        return wet * (-0.2 * t + 0.8 * s - 0.05 * t * t + 0.03 * t * s)

    def momentum(k, carry):
        above, above_h, sum_u, sum_v, star_u, star_v = carry
        level = k.astype(f32)
        wet_full = (sa[3, 0] > level).astype(f32)
        wet = (sa[3, 0, SUB:top, :] > level).astype(f32)
        wet_h = (sa[3, 1, SUB:top, :] > level).astype(f32)
        wet_up = (sa[3, 0, SUB + 1:top + 1, :] > level).astype(f32)
        rho = density(ext[0, k], ext[1, k], wet_full)
        above = above + rho
        pressure = thickness * (above - 0.5 * rho)
        rho_h = density(beside(0, k), beside(1, k), wet_h)
        above_h = above_h + rho_h
        pressure_h = thickness * (above_h - 0.5 * rho_h)
        pbuf[...] = pressure
        p = pbuf[SUB:top, :]
        grad_lon = 0.5 * (following(p, pressure_h) - right(jnp.where(lane == cols - 1, pressure_h, p), 1))
        grad_lat = 0.5 * (pbuf[SUB + 1:top + 1, :] - pbuf[SUB - 1:top - 1, :])
        u = ext[2, k, SUB:top, :]
        v = ext[3, k, SUB:top, :]
        s_lon = 0.5 * (u + following(u, beside(2, k))) * wet * following(wet, wet_h)
        s_lat = 0.5 * (v + ext[3, k, SUB + 1:top + 1, :]) * wet * wet_up
        speed_lon[k] = s_lon
        speed_lat[k] = s_lat
        accel_u = wet * (coriolis * v - advect(2, k, s_lon, s_lat) - grad_lon)
        accel_v = wet * (-advect(3, k, s_lon, s_lat) - coriolis * u - grad_lat)
        u_star = wet * u + tracer_step * accel_u
        v_star = wet * v + tracer_step * accel_v
        out[2, k] = u_star
        out[3, k] = v_star
        return above, above_h, sum_u + accel_u, sum_v + accel_v, star_u + u_star, star_v + v_star

    zero = jnp.zeros((rows, cols), f32)
    _, _, sum_u, sum_v, star_u, star_v = lax.fori_loop(
        0, nlev, momentum, (jnp.zeros((full, cols), f32), zero, zero, zero, zero, zero))
    per_depth = thickness / jnp.maximum(thickness * sa[3, 0, SUB:top, :], thickness)
    sf[0, 0, SUB:top, :] = sum_u * per_depth
    sf[1, 0, SUB:top, :] = sum_v * per_depth
    mean_star_u = star_u * per_depth
    mean_star_v = star_v * per_depth
    force_lon_pair.start()

    def tracers(k, carry):
        wet = (sa[3, 0, SUB:top, :] > k.astype(f32)).astype(f32)
        s_lon = speed_lon[k]
        s_lat = speed_lat[k]
        for q in range(2):
            out[q, k] = wet * (ext[q, k, SUB:top, :] - tracer_step * advect(q, k, s_lon, s_lat))
        return carry

    lax.fori_loop(0, nlev // 2, tracers, 0)
    force_lon_pair.wait_recv()
    close_lon(sf, sf_lon, 2)
    stage_north(sf, sf_north, (-1.0, -1.0))
    force_lat_pair.start()
    lax.fori_loop(nlev // 2, nlev, tracers, 0)
    force_lat_pair.wait_recv()

    def slope_lon(c, h):
        up_c = left(jnp.where(lane_full == 0, h, c), 1)
        up_h = left(jnp.where(lane_full == 0, c, h), 1)
        down_c = right(jnp.where(lane_full == cols - 1, h, c), 1)
        down_h = right(jnp.where(lane_full == cols - 1, c, h), 1)
        return 0.5 * (up_c - down_c), 0.5 * (up_h - down_h)

    def slope_lat(c, h):
        return tuple(0.5 * (pltpu.roll(a, full - 1, axis=0) - pltpu.roll(a, 1, axis=0)) for a in (c, h))

    both = (0, 1)
    height = [sa[0, i] for i in both]
    mean_u = [sa[1, i] for i in both]
    mean_v = [sa[2, i] for i in both]
    depth = [thickness * sa[3, i] for i in both]
    sea = [(sa[3, i] > 0.0).astype(f32) for i in both]
    for _ in range(NSUB):
        dx = slope_lon(*[depth[i] * mean_u[i] for i in both])
        dy = slope_lat(*[depth[i] * mean_v[i] for i in both])
        height = [sea[i] * (height[i] - surface_step * (dx[i] + dy[i])) for i in both]
        dx = slope_lon(*height)
        dy = slope_lat(*height)
        mean_u = [sea[i] * (mean_u[i] + surface_step * (sf[0, i] - dx[i])) for i in both]
        mean_v = [sea[i] * (mean_v[i] + surface_step * (sf[1, i] - dy[i])) for i in both]
    surf_out[0] = height[0][SUB:top]
    surf_out[1] = mean_u[0][SUB:top]
    surf_out[2] = mean_v[0][SUB:top]
    gain_u = mean_u[0][SUB:top] - mean_star_u
    gain_v = mean_v[0][SUB:top] - mean_star_v

    def finish(k, carry):
        wet = (sa[3, 0, SUB:top, :] > k.astype(f32)).astype(f32)
        out[2, k] = wet * (out[2, k] + gain_u)
        out[3, k] = wet * (out[3, k] + gain_v)
        return carry

    lax.fori_loop(0, nlev, finish, 0)

    for pair in (surf_lon, level_lon, level_lat, surf_lat, force_lon_pair, force_lat_pair):
        pair.wait_send()


def on_device(nx, ny, ocean_state, surface_state, column_levels):
    _, nlev, rows, cols = ocean_state.shape
    if cols % 128 or nlev * 8 > cols or nlev % 2 or rows % SUB or DEEP > SUB or nx % 2:
        raise ValueError("tile shape")
    full = rows + 2 * SUB
    vmem = pltpu.VMEM
    return pl.pallas_call(
        functools.partial(kernel, nx, ny),
        out_shape=(jax.ShapeDtypeStruct(ocean_state.shape, f32), jax.ShapeDtypeStruct(surface_state.shape, f32)),
        in_specs=[pl.BlockSpec(memory_space=pl.ANY), pl.BlockSpec(memory_space=vmem), pl.BlockSpec(memory_space=vmem)],
        out_specs=(pl.BlockSpec(memory_space=vmem), pl.BlockSpec(memory_space=vmem)),
        scratch_shapes=[
            vmem((4, nlev, full, cols), f32),
            vmem((4, rows, cols), f32),
            vmem((2, 4, rows, cols), f32),
            vmem((2, 2 * nlev, SUB, cols), f32),
            vmem((2, 2 * nlev, SUB, cols), f32),
            vmem((4, 2, full, cols), f32),
            vmem((2, 2, full, cols), f32),
            vmem((2, 4, rows, cols), f32),
            vmem((2, 2, rows, cols), f32),
            vmem((4, 2, SUB, cols), f32),
            vmem((2, 2, SUB, cols), f32),
            vmem((4, rows, cols), f32),
            vmem((4, nlev, cols), f32),
            vmem((nlev, rows, cols), f32),
            vmem((nlev, rows, cols), f32),
            vmem((full, cols), f32),
            vmem((full, cols), f32),
            pltpu.SemaphoreType.DMA,
            pltpu.SemaphoreType.DMA((12,)),
            pltpu.SemaphoreType.DMA((12,)),
        ],
        compiler_params=pltpu.CompilerParams(collective_id=0, has_side_effects=True,
                                             vmem_limit_bytes=32 * 1024 * 1024),
    )(ocean_state, surface_state, column_levels)


def solution(mesh):
    return jax.shard_map(
        functools.partial(on_device, mesh.shape["lon"], mesh.shape["lat"]),
        mesh=mesh,
        in_specs=(P(None, None, "lat", "lon"), P(None, "lat", "lon"), P("lat", "lon")),
        out_specs=(P(None, None, "lat", "lon"), P(None, "lat", "lon")),
        check_vma=False,
    )
```

time: 165 us -> 35.7 us (0.22)
  the two profiles are of different devices: /device:TPU:0 before, /device:TPU:3 now
where the time goes in v1:
time: 35.7 us; the launch traced here: 35.4 us
  Pallas kernels  30.4 us (85%)
  local copies, waits for them, and re-layouts  4.32 us (12%)
  between operations  0.65 us (2%)
    pallas_call x1, Pallas kernels, on_device(): pl.pallas_call(functools.partial(kernel, nx, ny), out_shape=(jax.ShapeDty...  30.4 us
    unnamed x8, local copies, waits for them, and re-layouts  4.32 us

profile of v1, /device:TPU:3, one launch (start us, length us, event | category | flops | bytes accessed | tf_op | source)
XLA Modules:
  0.0 35.4 jit_solution(5889058184335037269)
XLA Ops:
  0.6 0.0 copy-start
  0.6 1.2 %copy-done = f32[4,16,32,128]{3,2,1,0:T(8,128)S(1)} copy-done((f32[4,16,32,128]{3,2,1,0:T(8,128)S(1)}, f32[4,16,32,128]{3,2,1,0:T(8,128)}, u32[]{:S(2)}) %copy-start) | copy-done | bytes 1048600
  1.9 0.0 copy-start.1
  1.9 0.8 %copy-done.1 = f32[3,32,128]{2,1,0:T(8,128)S(1)} copy-done((f32[3,32,128]{2,1,0:T(8,128)S(1)}, f32[3,32,128]{2,1,0:T(8,128)}, u32[]{:S(2)}) %copy-start.1) | copy-done | bytes 49176
  2.7 0.0 copy-start.2
  2.7 0.7 %copy-done.2 = s32[32,128]{1,0:T(8,128)S(1)} copy-done((s32[32,128]{1,0:T(8,128)S(1)}, s32[32,128]{1,0:T(8,128)}, u32[]{:S(2)}) %copy-start.2) | copy-done | bytes 16408
  3.4 30.4 %shard_map.50 = (f32[4,16,32,128]{3,2,1,0:T(8,128)S(1)}, f32[3,32,128]{2,1,0:T(8,128)S(1)}) custom-call(f32[4,16,32,128]{3,2,1,0:T(8,128)S(1)} %copy-done, f32[3,32,128]{2,1,0:T(8,128)S(1)} %copy-done.1, s32[32,128]{1,0:T(8,128)S(1)} %copy-done.2), custom_call_target="tpu_custom_call" | custom-call | tf_op jit(solution)/shard_map/pallas_call | solution.py:399
  33.8 1.0 %copy.7 = f32[4,16,32,128]{3,2,1,0:T(8,128)} copy(f32[4,16,32,128]{3,2,1,0:T(8,128)S(1)} %get-tuple-element.4) | data formatting | bytes 2097152
  34.8 0.6 %copy.8 = f32[3,32,128]{2,1,0:T(8,128)} copy(f32[3,32,128]{2,1,0:T(8,128)S(1)} %get-tuple-element.5) | data formatting | bytes 98304
Async XLA Ops:
  0.6 1.2 %copy-start = (f32[4,16,32,128]{3,2,1,0:T(8,128)S(1)}, f32[4,16,32,128]{3,2,1,0:T(8,128)}, u32[]{:S(2)}) copy-start(f32[4,16,32,128]{3,2,1,0:T(8,128)} %ocean.1) | copy-start | bytes 3145732
  1.9 0.8 %copy-start.1 = (f32[3,32,128]{2,1,0:T(8,128)S(1)}, f32[3,32,128]{2,1,0:T(8,128)}, u32[]{:S(2)}) copy-start(f32[3,32,128]{2,1,0:T(8,128)} %surface.1) | copy-start | bytes 147460
  2.7 0.7 %copy-start.2 = (s32[32,128]{1,0:T(8,128)S(1)}, s32[32,128]{1,0:T(8,128)}, u32[]{:S(2)}) copy-start(s32[32,128]{1,0:T(8,128)} %levels_in.1) | copy-start | bytes 49156

commit v2 on v1

--- a/solution.py
+++ b/solution.py
@@ -19,6 +19,7 @@
 
 def face_flux(s, q0, q1, dm2, dm1, d0, dp1, dp2):
     pos = s >= 0.0
+    sixth = jnp.abs(s) * (1.0 / 6.0)
     c = jnp.where(pos, q0, q1)
     d1 = jnp.where(pos, dm2, dp2)
     d2 = jnp.where(pos, dm1, dp1)
@@ -41,10 +42,7 @@
     w2 = 6.0 * (p13 * p13)
     w3 = 3.0 * (p12 * p12)
     top = w1 * (2.0 * t1 - d2) + w2 * (t2 + d3) + w3 * (d3 - t3)
-    total = 6.0 * (w1 + w2 + w3)
-    r = pl.reciprocal(total, approx=True)
-    r = r * (2.0 - total * r)
-    return s * c + jnp.abs(s) * (top * r)
+    return s * c + sixth * (top * pl.reciprocal(w1 + w2 + w3, approx=True))
 
 
 def left(x, n):
@@ -55,9 +53,9 @@
     return pltpu.roll(x, n, axis=x.ndim - 1)
 
 
-def kernel(nx, ny, ocean, surface, levels_in, out, surf_out, ext, lon_own, lon_in, lat_out, lat_in, sa, sf,
+def kernel(nx, ny, ocean, surface, levels_in, out_hbm, surf_out, ext, lon_own, lon_in, lat_out, lat_in, sa, sf,
            sa_lon, sf_lon, sa_north, sf_north, extra_lon, extra_lat, speed_lon, speed_lat, pbuf, fbuf,
-           local_sem, send_sem, recv_sem):
+           flat, out, counts, local_sem, store_sem, send_sem, recv_sem):
     nlev, rows, cols = ocean.shape[1], ocean.shape[2], ocean.shape[3]
     top = SUB + rows
     full = top + SUB
@@ -73,11 +71,12 @@
     fold = jnp.where(at_north, 1, 0)
     far_row = pl.multiple_of(fold * top, SUB)
 
-    load = pltpu.make_async_copy(ocean, ext.at[:, :, SUB:top, :], local_sem)
+    load = pltpu.make_async_copy(ocean, ext.at[:, :, SUB:top, :], local_sem.at[0])
+    load_surface = pltpu.make_async_copy(surface, sa.at[0:3, 0, SUB:top, :], local_sem.at[1])
+    load_counts = pltpu.make_async_copy(levels_in, counts, local_sem.at[2])
     load.start()
-
-    sa[0:3, 0, SUB:top, :] = surface[...]
-    sa[3, 0, SUB:top, :] = levels_in[...].astype(f32)
+    load_surface.start()
+    load_counts.start()
 
     @pl.when(y == 0)
     def _():
@@ -92,8 +91,6 @@
     @pl.when(y > 0)
     def _():
         pl.semaphore_signal(barrier, inc=1, device_id=south, device_id_type=pl.DeviceIdType.MESH)
-
-    pl.semaphore_wait(barrier, 3 + jnp.where(y > 0, 1, 0))
 
     def remote(src, dst, send, recv, target):
         return pltpu.make_async_remote_copy(
@@ -152,8 +149,6 @@
                        sa.at[:, :, 0:SUB, :], sa.at[:, :, top:full, :], 8)
     force_lat_pair = LatPair(sf_north, sf.at[:, :, pl.ds(far_row, SUB), :], sf.at[:, :, SUB:2 * SUB, :],
                              sf.at[:, :, 0:SUB, :], sf.at[:, :, top:full, :], 10)
-
-    surf_lon.start()
 
     lane = lax.broadcasted_iota(jnp.int32, (rows, cols), 1)
     lane_full = lax.broadcasted_iota(jnp.int32, (full, cols), 1)
@@ -173,14 +168,6 @@
         return lax.dot(flip_rows, block, precision=lax.Precision.HIGHEST, preferred_element_type=f32)
 
     load.wait()
-
-    for q in range(4):
-        pack = jnp.zeros((rows, cols), f32)
-        for k in range(nlev):
-            pack = jnp.where(owner == k, right(ext[q, k, SUB:top, :], wide * k + 3), pack)
-        lon_own[q] = pack
-    level_lon.start()
-
     half = nlev // 2
     for q in range(4):
         for h in range(half):
@@ -198,7 +185,19 @@
             block = lat_out[0, q * half:(q + 1) * half].reshape(half * SUB, cols)
             lat_out[0, q * half:(q + 1) * half] = (sign * mirrored(block)).reshape(half, SUB, cols)
 
+    load_surface.wait()
+    load_counts.wait()
+    sa[3, 0, SUB:top, :] = counts[...].astype(f32)
+    pl.semaphore_wait(barrier, 3 + jnp.where(y > 0, 1, 0))
+    surf_lon.start()
     level_lat.start()
+
+    for q in range(4):
+        pack = jnp.zeros((rows, cols), f32)
+        for k in range(nlev):
+            pack = jnp.where(owner == k, right(ext[q, k, SUB:top, :], wide * k + 3), pack)
+        lon_own[q] = pack
+    level_lon.start()
 
     def close_lon(fields, arrived, count):
         for f in range(count):
@@ -220,6 +219,27 @@
     close_lon(sa, sa_lon, 4)
     stage_north(sa, sa_north, (1.0, -1.0, -1.0, 1.0))
     surf_lat.start()
+
+    def face_rows(q, k, s, first, count):
+        cell = [ext[q, k, first - 2 + i:first - 2 + i + count, :] for i in range(6)]
+        return face_flux(s, cell[2], cell[3], *[cell[i + 1] - cell[i] for i in range(5)])
+
+    def lat_speed(k, first, count):
+        level = k.astype(f32)
+        wet = (sa[3, 0, first:first + count, :] > level).astype(f32)
+        wet_up = (sa[3, 0, first + 1:first + 1 + count, :] > level).astype(f32)
+        return 0.5 * (ext[3, k, first:first + count, :] + ext[3, k, first + 1:first + 1 + count, :]) * wet * wet_up
+
+    inner, inner_count = 2 * SUB, rows - 2 * SUB
+
+    def inner_faces(i, carry):
+        for k in (2 * i, 2 * i + 1):
+            s = lat_speed(k, inner, inner_count)
+            for q in range(4):
+                flat[q, k] = face_rows(q, k, s, inner, inner_count)
+        return carry
+
+    lax.fori_loop(0, half, inner_faces, 0)
 
     level_lon.wait_recv()
     level_lat.wait_recv()
@@ -262,7 +282,7 @@
     def following(c, h):
         return left(jnp.where(lane == 0, h, c), 1)
 
-    def advect(q, k, s_lon, s_lat):
+    def advect(q, k, s_lon, s_south, s_north, slot):
         c = ext[q, k, SUB:top, :]
         h = beside(q, k)
         c1 = following(c, h)
@@ -277,12 +297,11 @@
             left(jnp.where(lane < 2, dh, d), 2))
         edge = pltpu.roll(extra_lon[q], cols - 2 - wide * k, axis=1)
         along = flux - jnp.where(lane == 0, edge, right(flux, 1))
-        cell = [ext[q, k, SUB - 2 + i:top - 2 + i, :] for i in range(6)]
-        d = [cell[i + 1] - cell[i] for i in range(5)]
-        flux = face_flux(s_lat, cell[2], cell[3], *d)
-        fbuf[SUB:top, :] = flux
-        fbuf[SUB - 1:SUB, :] = extra_lat[q, pl.ds(k, 1), :]
-        return along + (flux - fbuf[SUB - 1:top - 1, :])
+        fbuf[slot, SUB - 1:SUB, :] = extra_lat[q, pl.ds(k, 1), :]
+        fbuf[slot, SUB:2 * SUB, :] = face_rows(q, k, s_south, SUB, SUB)
+        fbuf[slot, inner:top - SUB, :] = flat[q, k]
+        fbuf[slot, top - SUB:top, :] = face_rows(q, k, s_north, top - SUB, SUB)
+        return along + (fbuf[slot, SUB:top, :] - fbuf[slot, SUB - 1:top - 1, :])
 
     row = lax.broadcasted_iota(jnp.int32, (rows, cols), 0)
     latitude = ((y * rows + row).astype(f32) + 0.5) / float(ny * rows)
@@ -291,40 +310,46 @@
     def density(t, s, wet):
         return wet * (-0.2 * t + 0.8 * s - 0.05 * t * t + 0.03 * t * s)
 
-    def momentum(k, carry):
+    def momentum_level(k, slot, carry):
         above, above_h, sum_u, sum_v, star_u, star_v = carry
         level = k.astype(f32)
         wet_full = (sa[3, 0] > level).astype(f32)
         wet = (sa[3, 0, SUB:top, :] > level).astype(f32)
         wet_h = (sa[3, 1, SUB:top, :] > level).astype(f32)
-        wet_up = (sa[3, 0, SUB + 1:top + 1, :] > level).astype(f32)
         rho = density(ext[0, k], ext[1, k], wet_full)
         above = above + rho
         pressure = thickness * (above - 0.5 * rho)
         rho_h = density(beside(0, k), beside(1, k), wet_h)
         above_h = above_h + rho_h
         pressure_h = thickness * (above_h - 0.5 * rho_h)
-        pbuf[...] = pressure
-        p = pbuf[SUB:top, :]
+        pbuf[slot] = pressure
+        p = pbuf[slot, SUB:top, :]
         grad_lon = 0.5 * (following(p, pressure_h) - right(jnp.where(lane == cols - 1, pressure_h, p), 1))
-        grad_lat = 0.5 * (pbuf[SUB + 1:top + 1, :] - pbuf[SUB - 1:top - 1, :])
+        grad_lat = 0.5 * (pbuf[slot, SUB + 1:top + 1, :] - pbuf[slot, SUB - 1:top - 1, :])
         u = ext[2, k, SUB:top, :]
         v = ext[3, k, SUB:top, :]
         s_lon = 0.5 * (u + following(u, beside(2, k))) * wet * following(wet, wet_h)
-        s_lat = 0.5 * (v + ext[3, k, SUB + 1:top + 1, :]) * wet * wet_up
+        s_south = lat_speed(k, SUB, SUB)
+        s_north = lat_speed(k, top - SUB, SUB)
         speed_lon[k] = s_lon
-        speed_lat[k] = s_lat
-        accel_u = wet * (coriolis * v - advect(2, k, s_lon, s_lat) - grad_lon)
-        accel_v = wet * (-advect(3, k, s_lon, s_lat) - coriolis * u - grad_lat)
+        speed_lat[0, k] = s_south
+        speed_lat[1, k] = s_north
+        accel_u = wet * (coriolis * v - advect(2, k, s_lon, s_south, s_north, 2 * slot) - grad_lon)
+        accel_v = wet * (-advect(3, k, s_lon, s_south, s_north, 2 * slot + 1) - coriolis * u - grad_lat)
         u_star = wet * u + tracer_step * accel_u
         v_star = wet * v + tracer_step * accel_v
         out[2, k] = u_star
         out[3, k] = v_star
         return above, above_h, sum_u + accel_u, sum_v + accel_v, star_u + u_star, star_v + v_star
 
+    def momentum(i, carry):
+        for slot in range(2):
+            carry = momentum_level(2 * i + slot, slot, carry)
+        return carry
+
     zero = jnp.zeros((rows, cols), f32)
     _, _, sum_u, sum_v, star_u, star_v = lax.fori_loop(
-        0, nlev, momentum, (jnp.zeros((full, cols), f32), zero, zero, zero, zero, zero))
+        0, half, momentum, (jnp.zeros((full, cols), f32), zero, zero, zero, zero, zero))
     per_depth = thickness / jnp.maximum(thickness * sa[3, 0, SUB:top, :], thickness)
     sf[0, 0, SUB:top, :] = sum_u * per_depth
     sf[1, 0, SUB:top, :] = sum_v * per_depth
@@ -332,20 +357,29 @@
     mean_star_v = star_v * per_depth
     force_lon_pair.start()
 
-    def tracers(k, carry):
-        wet = (sa[3, 0, SUB:top, :] > k.astype(f32)).astype(f32)
-        s_lon = speed_lon[k]
-        s_lat = speed_lat[k]
-        for q in range(2):
-            out[q, k] = wet * (ext[q, k, SUB:top, :] - tracer_step * advect(q, k, s_lon, s_lat))
+    def tracers(i, carry):
+        for slot in range(2):
+            k = 2 * i + slot
+            wet = (sa[3, 0, SUB:top, :] > k.astype(f32)).astype(f32)
+            for q in range(2):
+                change = advect(q, k, speed_lon[k], speed_lat[0, k], speed_lat[1, k], 2 * slot + q)
+                out[q, k] = wet * (ext[q, k, SUB:top, :] - tracer_step * change)
         return carry
 
-    lax.fori_loop(0, nlev // 2, tracers, 0)
+    def store(q, k0, k1, sem):
+        part = pltpu.make_async_copy(out.at[q:q + 2, k0:k1], out_hbm.at[q:q + 2, k0:k1], store_sem.at[sem])
+        part.start()
+        return part
+
+    mid = half // 2
+    lax.fori_loop(0, mid, tracers, 0)
     force_lon_pair.wait_recv()
     close_lon(sf, sf_lon, 2)
     stage_north(sf, sf_north, (-1.0, -1.0))
     force_lat_pair.start()
-    lax.fori_loop(nlev // 2, nlev, tracers, 0)
+    stores = [store(0, 0, 2 * mid, 0)]
+    lax.fori_loop(mid, half, tracers, 0)
+    stores.append(store(0, 2 * mid, nlev, 1))
     force_lat_pair.wait_recv()
 
     def slope_lon(c, h):
@@ -378,13 +412,18 @@
     gain_u = mean_u[0][SUB:top] - mean_star_u
     gain_v = mean_v[0][SUB:top] - mean_star_v
 
-    def finish(k, carry):
-        wet = (sa[3, 0, SUB:top, :] > k.astype(f32)).astype(f32)
-        out[2, k] = wet * (out[2, k] + gain_u)
-        out[3, k] = wet * (out[3, k] + gain_v)
-        return carry
-
-    lax.fori_loop(0, nlev, finish, 0)
+    def finish(k0, k1):
+        for k in range(k0, k1):
+            wet = (sa[3, 0, SUB:top, :] > k).astype(f32)
+            out[2, k] = wet * (out[2, k] + gain_u)
+            out[3, k] = wet * (out[3, k] + gain_v)
+
+    finish(0, half)
+    stores.append(store(2, 0, half, 2))
+    finish(half, nlev)
+    stores.append(store(2, half, nlev, 3))
+    for part in stores:
+        part.wait()
 
     for pair in (surf_lon, level_lon, level_lat, surf_lat, force_lon_pair, force_lat_pair):
         pair.wait_send()
@@ -392,15 +431,15 @@
 
 def on_device(nx, ny, ocean_state, surface_state, column_levels):
     _, nlev, rows, cols = ocean_state.shape
-    if cols % 128 or nlev * 8 > cols or nlev % 2 or rows % SUB or DEEP > SUB or nx % 2:
+    if cols % 128 or nlev * 8 > cols or nlev % 4 or rows % SUB or rows < 3 * SUB or DEEP > SUB or nx % 2:
         raise ValueError("tile shape")
     full = rows + 2 * SUB
     vmem = pltpu.VMEM
     return pl.pallas_call(
         functools.partial(kernel, nx, ny),
         out_shape=(jax.ShapeDtypeStruct(ocean_state.shape, f32), jax.ShapeDtypeStruct(surface_state.shape, f32)),
-        in_specs=[pl.BlockSpec(memory_space=pl.ANY), pl.BlockSpec(memory_space=vmem), pl.BlockSpec(memory_space=vmem)],
-        out_specs=(pl.BlockSpec(memory_space=vmem), pl.BlockSpec(memory_space=vmem)),
+        in_specs=[pl.BlockSpec(memory_space=pltpu.HBM)] * 3,
+        out_specs=(pl.BlockSpec(memory_space=pl.ANY), pl.BlockSpec(memory_space=vmem)),
         scratch_shapes=[
             vmem((4, nlev, full, cols), f32),
             vmem((4, rows, cols), f32),
@@ -416,15 +455,18 @@
             vmem((4, rows, cols), f32),
             vmem((4, nlev, cols), f32),
             vmem((nlev, rows, cols), f32),
-            vmem((nlev, rows, cols), f32),
-            vmem((full, cols), f32),
-            vmem((full, cols), f32),
-            pltpu.SemaphoreType.DMA,
+            vmem((2, nlev, SUB, cols), f32),
+            vmem((2, full, cols), f32),
+            vmem((4, full, cols), f32),
+            vmem((4, nlev, rows - 2 * SUB, cols), f32),
+            vmem((4, nlev, rows, cols), f32),
+            vmem((rows, cols), jnp.int32),
+            pltpu.SemaphoreType.DMA((3,)),
+            pltpu.SemaphoreType.DMA((4,)),
             pltpu.SemaphoreType.DMA((12,)),
             pltpu.SemaphoreType.DMA((12,)),
         ],
-        compiler_params=pltpu.CompilerParams(collective_id=0, has_side_effects=True,
-                                             vmem_limit_bytes=32 * 1024 * 1024),
+        compiler_params=pltpu.CompilerParams(collective_id=0, has_side_effects=True),
     )(ocean_state, surface_state, column_levels)
 
 

time: 35.7 us -> 31.7 us (0.89)
  the two profiles are of different devices: /device:TPU:3 before, /device:TPU:1 now
where the time goes in v2:
time: 31.7 us; the launch traced here: 31.5 us
  Pallas kernels  28 us (88%)
  local copies, waits for them, and re-layouts  2.9 us (9%)
  between operations  0.65 us (2%)
    pallas_call x1, Pallas kernels, on_device(): pl.pallas_call(functools.partial(kernel, nx, ny), out_shape=(jax.ShapeDty...  28 us
    unnamed x4, local copies, waits for them, and re-layouts  2.9 us

profile of v2, /device:TPU:1, one launch (start us, length us, event | category | flops | bytes accessed | tf_op | source)
XLA Modules:
  0.0 31.5 jit_solution(14025857034755018093)
XLA Ops:
  0.6 28.0 %shard_map.50 = (f32[4,16,32,128]{3,2,1,0:T(8,128)}, f32[3,32,128]{2,1,0:T(8,128)}) custom-call(f32[4,16,32,128]{3,2,1,0:T(8,128)} %ocean.1, f32[3,32,128]{2,1,0:T(8,128)} %surface.1, s32[32,128]{1,0:T(8,128)} %levels_in.1), custom_call_target="tpu_custom_call" | custom-call | tf_op jit(solution)/shard_map/pallas_call | solution.py:438
  28.6 0.0 copy-start
  28.6 2.3 %copy.7 = f32[4,16,32,128]{3,2,1,0:T(8,128)} copy(f32[4,16,32,128]{3,2,1,0:T(8,128)} %get-tuple-element.4) | data formatting | bytes 2097152
  30.9 0.0 copy-done
  30.9 0.6 %copy.8 = f32[3,32,128]{2,1,0:T(8,128)} copy(f32[3,32,128]{2,1,0:T(8,128)S(1)} %copy-done) | data formatting | bytes 98304
Async XLA Ops:
  28.6 2.3 %copy-start = (f32[3,32,128]{2,1,0:T(8,128)S(1)}, f32[3,32,128]{2,1,0:T(8,128)}, u32[]{:S(2)}) copy-start(f32[3,32,128]{2,1,0:T(8,128)} %get-tuple-element.5) | copy-start | bytes 147460

commit v3 on v2

--- a/solution.py
+++ b/solution.py
@@ -53,7 +53,7 @@
     return pltpu.roll(x, n, axis=x.ndim - 1)
 
 
-def kernel(nx, ny, ocean, surface, levels_in, out_hbm, surf_out, ext, lon_own, lon_in, lat_out, lat_in, sa, sf,
+def kernel(nx, ny, ocean, surface, levels_in, out_hbm, gain, surf_out, ext, lon_own, lon_in, lat_out, lat_in, sa, sf,
            sa_lon, sf_lon, sa_north, sf_north, extra_lon, extra_lat, speed_lon, speed_lat, pbuf, fbuf,
            flat, out, counts, local_sem, store_sem, send_sem, recv_sem):
     nlev, rows, cols = ocean.shape[1], ocean.shape[2], ocean.shape[3]
@@ -221,7 +221,8 @@
     surf_lat.start()
 
     def face_rows(q, k, s, first, count):
-        cell = [ext[q, k, first - 2 + i:first - 2 + i + count, :] for i in range(6)]
+        start = first - 2 + jnp.minimum(k, 0)
+        cell = [ext[q, k, pl.ds(start + i, count), :] for i in range(6)]
         return face_flux(s, cell[2], cell[3], *[cell[i + 1] - cell[i] for i in range(5)])
 
     def lat_speed(k, first, count):
@@ -357,6 +358,13 @@
     mean_star_v = star_v * per_depth
     force_lon_pair.start()
 
+    def store(q, k0, k1, sem):
+        part = pltpu.make_async_copy(out.at[q:q + 2, k0:k1], out_hbm.at[q:q + 2, k0:k1], store_sem.at[sem])
+        part.start()
+        return part
+
+    stores = [store(2, 0, nlev, 0)]
+
     def tracers(i, carry):
         for slot in range(2):
             k = 2 * i + slot
@@ -366,20 +374,15 @@
                 out[q, k] = wet * (ext[q, k, SUB:top, :] - tracer_step * change)
         return carry
 
-    def store(q, k0, k1, sem):
-        part = pltpu.make_async_copy(out.at[q:q + 2, k0:k1], out_hbm.at[q:q + 2, k0:k1], store_sem.at[sem])
-        part.start()
-        return part
-
     mid = half // 2
     lax.fori_loop(0, mid, tracers, 0)
     force_lon_pair.wait_recv()
     close_lon(sf, sf_lon, 2)
     stage_north(sf, sf_north, (-1.0, -1.0))
     force_lat_pair.start()
-    stores = [store(0, 0, 2 * mid, 0)]
+    stores.append(store(0, 0, 2 * mid, 1))
     lax.fori_loop(mid, half, tracers, 0)
-    stores.append(store(0, 2 * mid, nlev, 1))
+    stores.append(store(0, 2 * mid, nlev, 2))
     force_lat_pair.wait_recv()
 
     def slope_lon(c, h):
@@ -409,19 +412,10 @@
     surf_out[0] = height[0][SUB:top]
     surf_out[1] = mean_u[0][SUB:top]
     surf_out[2] = mean_v[0][SUB:top]
-    gain_u = mean_u[0][SUB:top] - mean_star_u
-    gain_v = mean_v[0][SUB:top] - mean_star_v
-
-    def finish(k0, k1):
-        for k in range(k0, k1):
-            wet = (sa[3, 0, SUB:top, :] > k).astype(f32)
-            out[2, k] = wet * (out[2, k] + gain_u)
-            out[3, k] = wet * (out[3, k] + gain_v)
-
-    finish(0, half)
-    stores.append(store(2, 0, half, 2))
-    finish(half, nlev)
-    stores.append(store(2, half, nlev, 3))
+    gain[0] = zero
+    gain[1] = zero
+    gain[2] = mean_u[0][SUB:top] - mean_star_u
+    gain[3] = mean_v[0][SUB:top] - mean_star_v
     for part in stores:
         part.wait()
 
@@ -435,11 +429,12 @@
         raise ValueError("tile shape")
     full = rows + 2 * SUB
     vmem = pltpu.VMEM
-    return pl.pallas_call(
+    stars, gain, surface_next = pl.pallas_call(
         functools.partial(kernel, nx, ny),
-        out_shape=(jax.ShapeDtypeStruct(ocean_state.shape, f32), jax.ShapeDtypeStruct(surface_state.shape, f32)),
+        out_shape=(jax.ShapeDtypeStruct(ocean_state.shape, f32), jax.ShapeDtypeStruct((4, rows, cols), f32),
+                   jax.ShapeDtypeStruct(surface_state.shape, f32)),
         in_specs=[pl.BlockSpec(memory_space=pltpu.HBM)] * 3,
-        out_specs=(pl.BlockSpec(memory_space=pl.ANY), pl.BlockSpec(memory_space=vmem)),
+        out_specs=(pl.BlockSpec(memory_space=pl.ANY), pl.BlockSpec(memory_space=vmem), pl.BlockSpec(memory_space=vmem)),
         scratch_shapes=[
             vmem((4, nlev, full, cols), f32),
             vmem((4, rows, cols), f32),
@@ -462,12 +457,14 @@
             vmem((4, nlev, rows, cols), f32),
             vmem((rows, cols), jnp.int32),
             pltpu.SemaphoreType.DMA((3,)),
-            pltpu.SemaphoreType.DMA((4,)),
+            pltpu.SemaphoreType.DMA((3,)),
             pltpu.SemaphoreType.DMA((12,)),
             pltpu.SemaphoreType.DMA((12,)),
         ],
         compiler_params=pltpu.CompilerParams(collective_id=0, has_side_effects=True),
     )(ocean_state, surface_state, column_levels)
+    level = lax.broadcasted_iota(jnp.int32, stars.shape, 1)
+    return jnp.where(level < column_levels, stars + gain[:, None], 0.0), surface_next
 
 
 def solution(mesh):

time: 31.7 us -> 31 us (0.978)
  other arithmetic: 0 us -> 2.35 us
  local copies, waits for them, and re-layouts: 2.9 us -> 0.63 us
  Pallas kernels: 28 us -> 27.2 us
    select_n x0 -> x1, other arithmetic: none -> 2.35 us  [on_device(): jnp.where(level < column_levels, stars + gain[:, None], 0.0)]
    unnamed x4 -> x5, local copies, waits for them, and re-layouts: 2.9 us -> 0.63 us
    pallas_call x1, Pallas kernels: 28 us -> 27.2 us  [on_device(): pl.pallas_call(functools.partial(kernel, nx, ny), out_shape=(jax.ShapeDty...]
where the time goes in v3:
time: 31 us; the launch traced here: 30.8 us
  Pallas kernels  27.2 us (88%)
  other arithmetic  2.35 us (8%)
  between operations  0.66 us (2%)
  local copies, waits for them, and re-layouts  0.63 us (2%)
    pallas_call x1, Pallas kernels, on_device(): pl.pallas_call(functools.partial(kernel, nx, ny), out_shape=(jax.ShapeDty...  27.2 us
    select_n x1, other arithmetic, on_device(): jnp.where(level < column_levels, stars + gain[:, None], 0.0)  2.35 us
    unnamed x5, local copies, waits for them, and re-layouts  0.63 us

profile of v3, /device:TPU:1, one launch (start us, length us, event | category | flops | bytes accessed | tf_op | source)
XLA Modules:
  0.0 30.8 jit_solution(9786149144712275512)
XLA Ops:
  0.6 0.0 copy-start
  0.6 27.2 %shard_map.50 = (f32[4,16,32,128]{3,2,1,0:T(8,128)}, f32[4,32,128]{2,1,0:T(8,128)}, f32[3,32,128]{2,1,0:T(8,128)}) custom-call(f32[4,16,32,128]{3,2,1,0:T(8,128)} %ocean.1, f32[3,32,128]{2,1,0:T(8,128)} %surface.1, s32[32,128]{1,0:T(8,128)} %levels_in.1), custom_call_target="tpu_custom_call" | custom-call | tf_op jit(solution)/shard_map/pallas_call | solution.py:432
  27.9 0.0 copy-done
  27.9 0.0 copy-start.1
  27.9 2.4 %add_select_fusion = f32[4,16,32,128]{3,2,1,0:T(8,128)} fusion(f32[4,16,32,128]{3,2,1,0:T(8,128)} %get-tuple-element.5, f32[4,32,128]{2,1,0:T(8,128)} %get-tuple-element.6, s32[32,128]{1,0:T(8,128)S(1)} %copy-done), kind=kLoop, calls=%fused_computation | loop fusion | flops 786432 | bytes 2179072 | tf_op jit(solution)/shard_map/jit(_where)/select_n | solution.py:467
  30.2 0.0 copy-done.1
  30.2 0.6 %copy.6 = f32[3,32,128]{2,1,0:T(8,128)} copy(f32[3,32,128]{2,1,0:T(8,128)S(1)} %copy-done.1) | data formatting | bytes 98304
Async XLA Ops:
  0.6 27.2 %copy-start = (s32[32,128]{1,0:T(8,128)S(1)}, s32[32,128]{1,0:T(8,128)}, u32[]{:S(2)}) copy-start(s32[32,128]{1,0:T(8,128)} %levels_in.1) | copy-start | bytes 49156
  27.9 2.4 %copy-start.1 = (f32[3,32,128]{2,1,0:T(8,128)S(1)}, f32[3,32,128]{2,1,0:T(8,128)}, u32[]{:S(2)}) copy-start(f32[3,32,128]{2,1,0:T(8,128)} %get-tuple-element.11) | copy-start | bytes 147460

commit v4 on v3

--- a/solution.py
+++ b/solution.py
@@ -19,30 +19,30 @@
 
 def face_flux(s, q0, q1, dm2, dm1, d0, dp1, dp2):
     pos = s >= 0.0
-    sixth = jnp.abs(s) * (1.0 / 6.0)
+    third = jnp.abs(s) * (1.0 / 3.0)
     c = jnp.where(pos, q0, q1)
     d1 = jnp.where(pos, dm2, dp2)
     d2 = jnp.where(pos, dm1, dp1)
     d3 = d0
     d4 = jnp.where(pos, dp1, dm1)
-    k = 13.0 / 3.0
-    b1 = d2 - d1
-    b2 = d3 - d2
-    b3 = d4 - d3
-    t1 = 3.0 * d2 - d1
-    t2 = d2 + d3
-    t3 = d4 - 3.0 * d3
-    s1 = (k * b1) * b1 + t1 * t1 + 4.0 * epsilon
-    s2 = (k * b2) * b2 + t2 * t2 + 4.0 * epsilon
-    s3 = (k * b3) * b3 + t3 * t3 + 4.0 * epsilon
+    rest2 = ((39.0 / 64.0) * d2) * d2 + 0.75 * epsilon
+    rest3 = ((39.0 / 64.0) * d3) * d3 + 0.75 * epsilon
+    g1 = d1 - (11.0 / 8.0) * d2
+    g2 = d2 - (5.0 / 8.0) * d3
+    g3 = d4 - (11.0 / 8.0) * d3
+    s1 = g1 * g1 + rest2
+    s2 = g2 * g2 + rest3
+    s3 = g3 * g3 + rest3
     p23 = s2 * s3
     p13 = s1 * s3
     p12 = s1 * s2
-    w1 = p23 * p23
-    w2 = 6.0 * (p13 * p13)
-    w3 = 3.0 * (p12 * p12)
-    top = w1 * (2.0 * t1 - d2) + w2 * (t2 + d3) + w3 * (d3 - t3)
-    return s * c + sixth * (top * pl.reciprocal(w1 + w2 + w3, approx=True))
+    w1 = (p23 * (1.0 / 3.0)) * p23
+    w2 = p13 * p13
+    w3 = p12 * p12
+    twice = d3 + d3
+    top = w1 * (2.5 * d2 - d1) + w2 * (d2 + twice) + w3 * (twice - 0.5 * d4)
+    total = (w1 + w2) + (w2 + w3)
+    return s * c + third * (top * pl.reciprocal(total, approx=True))
 
 
 def left(x, n):
@@ -55,7 +55,7 @@
 
 def kernel(nx, ny, ocean, surface, levels_in, out_hbm, gain, surf_out, ext, lon_own, lon_in, lat_out, lat_in, sa, sf,
            sa_lon, sf_lon, sa_north, sf_north, extra_lon, extra_lat, speed_lon, speed_lat, pbuf, fbuf,
-           flat, out, counts, local_sem, store_sem, send_sem, recv_sem):
+           flat, out, counts, crow, lon_both, local_sem, store_sem, send_sem, recv_sem):
     nlev, rows, cols = ocean.shape[1], ocean.shape[2], ocean.shape[3]
     top = SUB + rows
     full = top + SUB
@@ -157,15 +157,16 @@
     sub8 = lax.broadcasted_iota(jnp.int32, (SUB, cols), 0)
 
     def mirrored(block):
-        count = block.shape[0]
-        a = lax.broadcasted_iota(jnp.int32, (cols, cols), 0)
-        b = lax.broadcasted_iota(jnp.int32, (cols, cols), 1)
-        flip_cols = (a + b == cols - 1).astype(f32)
-        a = lax.broadcasted_iota(jnp.int32, (count, count), 0)
-        b = lax.broadcasted_iota(jnp.int32, (count, count), 1)
-        flip_rows = ((a // SUB == b // SUB) & (a % SUB + b % SUB == SUB - 1)).astype(f32)
-        block = lax.dot(block, flip_cols, precision=lax.Precision.HIGHEST, preferred_element_type=f32)
-        return lax.dot(flip_rows, block, precision=lax.Precision.HIGHEST, preferred_element_type=f32)
+        for axis, length in ((0, SUB), (1, cols)):
+            at = lax.broadcasted_iota(jnp.int32, block.shape, axis)
+            size = block.shape[axis]
+            step = 1
+            while step < length:
+                up = pltpu.roll(block, step, axis=axis)
+                down = pltpu.roll(block, size - step, axis=axis)
+                block = jnp.where((at // step) % 2 == 1, up, down)
+                step *= 2
+        return block
 
     load.wait()
     half = nlev // 2
@@ -178,16 +179,21 @@
             s1 = ext[q, 2 * h + 1, SUB:2 * SUB, :]
             lat_out[1, q * half + h] = jnp.where(sub8 < 4, s0, pltpu.roll(s1, 4, axis=0))
 
+    load_surface.wait()
+    load_counts.wait()
+    sa[3, 0, SUB:top, :] = counts[...].astype(f32)
+    crow[SUB:top, :] = sa[3, 0, SUB:top, :]
+    lat_out[0, 4 * half] = crow[top - SUB:top, :]
+    lat_out[1, 4 * half] = crow[SUB:2 * SUB, :]
+
     @pl.when(at_north)
     def _():
+        lat_out[0, 4 * half] = mirrored(lat_out[0, 4 * half])
         for q in range(4):
             sign = 1.0 if q < 2 else -1.0
             block = lat_out[0, q * half:(q + 1) * half].reshape(half * SUB, cols)
             lat_out[0, q * half:(q + 1) * half] = (sign * mirrored(block)).reshape(half, SUB, cols)
 
-    load_surface.wait()
-    load_counts.wait()
-    sa[3, 0, SUB:top, :] = counts[...].astype(f32)
     pl.semaphore_wait(barrier, 3 + jnp.where(y > 0, 1, 0))
     surf_lon.start()
     level_lat.start()
@@ -215,21 +221,15 @@
                 block = staged[f].reshape(2 * SUB, cols)
                 staged[f] = (signs[f] * mirrored(block)).reshape(2, SUB, cols)
 
-    surf_lon.wait_recv()
-    close_lon(sa, sa_lon, 4)
-    stage_north(sa, sa_north, (1.0, -1.0, -1.0, 1.0))
-    surf_lat.start()
-
     def face_rows(q, k, s, first, count):
         start = first - 2 + jnp.minimum(k, 0)
         cell = [ext[q, k, pl.ds(start + i, count), :] for i in range(6)]
         return face_flux(s, cell[2], cell[3], *[cell[i + 1] - cell[i] for i in range(5)])
 
     def lat_speed(k, first, count):
-        level = k.astype(f32)
-        wet = (sa[3, 0, first:first + count, :] > level).astype(f32)
-        wet_up = (sa[3, 0, first + 1:first + 1 + count, :] > level).astype(f32)
-        return 0.5 * (ext[3, k, first:first + count, :] + ext[3, k, first + 1:first + 1 + count, :]) * wet * wet_up
+        least = jnp.minimum(crow[first:first + count, :], crow[first + 1:first + 1 + count, :])
+        speed = 0.5 * (ext[3, k, first:first + count, :] + ext[3, k, first + 1:first + 1 + count, :])
+        return jnp.where(least > k.astype(f32), speed, 0.0)
 
     inner, inner_count = 2 * SUB, rows - 2 * SUB
 
@@ -242,9 +242,15 @@
 
     lax.fori_loop(0, half, inner_faces, 0)
 
+    surf_lon.wait_recv()
+    close_lon(sa, sa_lon, 4)
+    stage_north(sa, sa_north, (1.0, -1.0, -1.0, 1.0))
+    surf_lat.start()
+
     level_lon.wait_recv()
     level_lat.wait_recv()
-    surf_lat.wait_recv()
+    crow[0:SUB, :] = lat_in[0, 4 * half]
+    crow[top:full, :] = lat_in[1, 4 * half]
 
     for q in range(4):
         for h in range(half):
@@ -256,9 +262,11 @@
     def lon_pack(q):
         return jnp.where(spot < 3, lon_in[0, q], lon_own[q])
 
-    count_here = sa[3, 0, SUB:top, :]
+    count_here = crow[SUB:top, :]
     count_beside = sa[3, 1, SUB:top, :]
     level_of = owner.astype(f32)
+    for q in range(4):
+        lon_both[q] = jnp.where(spot < 3, lon_in[0, q], lon_in[1, q])
     edge_wet = ((count_beside[:, cols - 1:cols] > level_of) & (count_here[:, 0:1] > level_of)).astype(f32)
     pack_u = lon_pack(2)
     edge_speed = 0.5 * (pack_u + left(pack_u, 1)) * edge_wet
@@ -269,7 +277,7 @@
                                  left(d, 2))
 
     level_row = lax.broadcasted_iota(jnp.int32, (nlev, cols), 0).astype(f32)
-    row_wet = ((sa[3, 0, SUB - 1:SUB, :] > level_row) & (sa[3, 0, SUB:SUB + 1, :] > level_row)).astype(f32)
+    row_wet = ((crow[SUB - 1:SUB, :] > level_row) & (crow[SUB:SUB + 1, :] > level_row)).astype(f32)
     row_speed = 0.5 * (ext[3, :, SUB - 1, :] + ext[3, :, SUB, :]) * row_wet
     for q in range(4):
         cell = [ext[q, :, SUB - 3 + i, :] for i in range(6)]
@@ -277,8 +285,7 @@
         extra_lat[q] = face_flux(row_speed, cell[2], cell[3], *d)
 
     def beside(q, k):
-        both = jnp.where(spot < 3, lon_in[0, q], lon_in[1, q])
-        return pltpu.roll(both, cols - 3 - wide * k, axis=1)
+        return pltpu.roll(lon_both[q], cols - 3 - wide * k, axis=1)
 
     def following(c, h):
         return left(jnp.where(lane == 0, h, c), 1)
@@ -311,25 +318,32 @@
     def density(t, s, wet):
         return wet * (-0.2 * t + 0.8 * s - 0.05 * t * t + 0.03 * t * s)
 
+    beside_wet = jnp.where(spot < 3, count_beside[:, cols - 1:cols], count_beside[:, 0:1]) > level_of
+    rho_beside = density(lon_both[0], lon_both[1], beside_wet.astype(f32))
+    total_beside = rho_beside
+    step = 1
+    while step < nlev:
+        total_beside = total_beside + jnp.where(owner >= step, right(total_beside, wide * step), 0.0)
+        step *= 2
+    lon_both[4] = thickness * (total_beside - 0.5 * rho_beside)
+    least_lon = jnp.minimum(count_here, following(count_here, count_beside))
+
     def momentum_level(k, slot, carry):
-        above, above_h, sum_u, sum_v, star_u, star_v = carry
+        above, sum_u, sum_v, star_u, star_v = carry
         level = k.astype(f32)
-        wet_full = (sa[3, 0] > level).astype(f32)
-        wet = (sa[3, 0, SUB:top, :] > level).astype(f32)
-        wet_h = (sa[3, 1, SUB:top, :] > level).astype(f32)
+        wet_full = (crow[...] > level).astype(f32)
+        wet = (crow[SUB:top, :] > level).astype(f32)
         rho = density(ext[0, k], ext[1, k], wet_full)
         above = above + rho
         pressure = thickness * (above - 0.5 * rho)
-        rho_h = density(beside(0, k), beside(1, k), wet_h)
-        above_h = above_h + rho_h
-        pressure_h = thickness * (above_h - 0.5 * rho_h)
+        pressure_h = beside(4, k)
         pbuf[slot] = pressure
         p = pbuf[slot, SUB:top, :]
         grad_lon = 0.5 * (following(p, pressure_h) - right(jnp.where(lane == cols - 1, pressure_h, p), 1))
         grad_lat = 0.5 * (pbuf[slot, SUB + 1:top + 1, :] - pbuf[slot, SUB - 1:top - 1, :])
         u = ext[2, k, SUB:top, :]
         v = ext[3, k, SUB:top, :]
-        s_lon = 0.5 * (u + following(u, beside(2, k))) * wet * following(wet, wet_h)
+        s_lon = jnp.where(least_lon > level, 0.5 * (u + following(u, beside(2, k))), 0.0)
         s_south = lat_speed(k, SUB, SUB)
         s_north = lat_speed(k, top - SUB, SUB)
         speed_lon[k] = s_lon
@@ -341,7 +355,7 @@
         v_star = wet * v + tracer_step * accel_v
         out[2, k] = u_star
         out[3, k] = v_star
-        return above, above_h, sum_u + accel_u, sum_v + accel_v, star_u + u_star, star_v + v_star
+        return above, sum_u + accel_u, sum_v + accel_v, star_u + u_star, star_v + v_star
 
     def momentum(i, carry):
         for slot in range(2):
@@ -349,9 +363,9 @@
         return carry
 
     zero = jnp.zeros((rows, cols), f32)
-    _, _, sum_u, sum_v, star_u, star_v = lax.fori_loop(
-        0, half, momentum, (jnp.zeros((full, cols), f32), zero, zero, zero, zero, zero))
-    per_depth = thickness / jnp.maximum(thickness * sa[3, 0, SUB:top, :], thickness)
+    _, sum_u, sum_v, star_u, star_v = lax.fori_loop(
+        0, half, momentum, (jnp.zeros((full, cols), f32), zero, zero, zero, zero))
+    per_depth = thickness / jnp.maximum(thickness * count_here, thickness)
     sf[0, 0, SUB:top, :] = sum_u * per_depth
     sf[1, 0, SUB:top, :] = sum_v * per_depth
     mean_star_u = star_u * per_depth
@@ -368,7 +382,7 @@
     def tracers(i, carry):
         for slot in range(2):
             k = 2 * i + slot
-            wet = (sa[3, 0, SUB:top, :] > k.astype(f32)).astype(f32)
+            wet = (crow[SUB:top, :] > k.astype(f32)).astype(f32)
             for q in range(2):
                 change = advect(q, k, speed_lon[k], speed_lat[0, k], speed_lat[1, k], 2 * slot + q)
                 out[q, k] = wet * (ext[q, k, SUB:top, :] - tracer_step * change)
@@ -383,6 +397,7 @@
     stores.append(store(0, 0, 2 * mid, 1))
     lax.fori_loop(mid, half, tracers, 0)
     stores.append(store(0, 2 * mid, nlev, 2))
+    surf_lat.wait_recv()
     force_lat_pair.wait_recv()
 
     def slope_lon(c, h):
@@ -439,8 +454,8 @@
             vmem((4, nlev, full, cols), f32),
             vmem((4, rows, cols), f32),
             vmem((2, 4, rows, cols), f32),
-            vmem((2, 2 * nlev, SUB, cols), f32),
-            vmem((2, 2 * nlev, SUB, cols), f32),
+            vmem((2, 2 * nlev + 1, SUB, cols), f32),
+            vmem((2, 2 * nlev + 1, SUB, cols), f32),
             vmem((4, 2, full, cols), f32),
             vmem((2, 2, full, cols), f32),
             vmem((2, 4, rows, cols), f32),
@@ -456,6 +471,8 @@
             vmem((4, nlev, rows - 2 * SUB, cols), f32),
             vmem((4, nlev, rows, cols), f32),
             vmem((rows, cols), jnp.int32),
+            vmem((full, cols), f32),
+            vmem((5, rows, cols), f32),
             pltpu.SemaphoreType.DMA((3,)),
             pltpu.SemaphoreType.DMA((3,)),
             pltpu.SemaphoreType.DMA((12,)),

time: 31 us -> 30.8 us (level)
  no operation moved by 1% of the time
where the time goes in v4:
time: 30.8 us; the launch traced here: 30.6 us
  Pallas kernels  27 us (88%)
  other arithmetic  2.35 us (8%)
  between operations  0.66 us (2%)
  local copies, waits for them, and re-layouts  0.63 us (2%)
    pallas_call x1, Pallas kernels, on_device(): pl.pallas_call(functools.partial(kernel, nx, ny), out_shape=(jax.ShapeDty...  27 us
    select_n x1, other arithmetic, on_device(): jnp.where(level < column_levels, stars + gain[:, None], 0.0)  2.35 us
    unnamed x5, local copies, waits for them, and re-layouts  0.63 us

profile of v4, /device:TPU:1, one launch (start us, length us, event | category | flops | bytes accessed | tf_op | source)
XLA Modules:
  0.0 30.6 jit_solution(12522285473311257825)
XLA Ops:
  0.6 0.0 copy-start
  0.6 27.0 %shard_map.50 = (f32[4,16,32,128]{3,2,1,0:T(8,128)}, f32[4,32,128]{2,1,0:T(8,128)}, f32[3,32,128]{2,1,0:T(8,128)}) custom-call(f32[4,16,32,128]{3,2,1,0:T(8,128)} %ocean.1, f32[3,32,128]{2,1,0:T(8,128)} %surface.1, s32[32,128]{1,0:T(8,128)} %levels_in.1), custom_call_target="tpu_custom_call" | custom-call | tf_op jit(solution)/shard_map/pallas_call | solution.py:447
  27.6 0.0 copy-done
  27.6 0.0 copy-start.1
  27.6 2.4 %add_select_fusion = f32[4,16,32,128]{3,2,1,0:T(8,128)} fusion(f32[4,16,32,128]{3,2,1,0:T(8,128)} %get-tuple-element.5, f32[4,32,128]{2,1,0:T(8,128)} %get-tuple-element.6, s32[32,128]{1,0:T(8,128)S(1)} %copy-done), kind=kLoop, calls=%fused_computation | loop fusion | flops 786432 | bytes 2179072 | tf_op jit(solution)/shard_map/jit(_where)/select_n | solution.py:484
  30.0 0.0 copy-done.1
  30.0 0.6 %copy.6 = f32[3,32,128]{2,1,0:T(8,128)} copy(f32[3,32,128]{2,1,0:T(8,128)S(1)} %copy-done.1) | data formatting | bytes 98304
Async XLA Ops:
  0.6 27.0 %copy-start = (s32[32,128]{1,0:T(8,128)S(1)}, s32[32,128]{1,0:T(8,128)}, u32[]{:S(2)}) copy-start(s32[32,128]{1,0:T(8,128)} %levels_in.1) | copy-start | bytes 49156
  27.6 2.4 %copy-start.1 = (f32[3,32,128]{2,1,0:T(8,128)S(1)}, f32[3,32,128]{2,1,0:T(8,128)}, u32[]{:S(2)}) copy-start(f32[3,32,128]{2,1,0:T(8,128)} %get-tuple-element.11) | copy-start | bytes 147460

commit v5 on v4

--- a/solution.py
+++ b/solution.py
@@ -195,8 +195,8 @@
             lat_out[0, q * half:(q + 1) * half] = (sign * mirrored(block)).reshape(half, SUB, cols)
 
     pl.semaphore_wait(barrier, 3 + jnp.where(y > 0, 1, 0))
+    level_lat.start()
     surf_lon.start()
-    level_lat.start()
 
     for q in range(4):
         pack = jnp.zeros((rows, cols), f32)
@@ -248,16 +248,6 @@
     surf_lat.start()
 
     level_lon.wait_recv()
-    level_lat.wait_recv()
-    crow[0:SUB, :] = lat_in[0, 4 * half]
-    crow[top:full, :] = lat_in[1, 4 * half]
-
-    for q in range(4):
-        for h in range(half):
-            for side, place in ((0, 0), (1, top)):
-                block = lat_in[side, q * half + h]
-                ext[q, 2 * h, place:place + SUB, :] = block
-                ext[q, 2 * h + 1, place:place + SUB, :] = pltpu.roll(block, 4, axis=0)
 
     def lon_pack(q):
         return jnp.where(spot < 3, lon_in[0, q], lon_own[q])
@@ -276,21 +266,13 @@
         extra_lon[q] = face_flux(edge_speed, pack, left(pack, 1), right(d, 2), right(d, 1), d, left(d, 1),
                                  left(d, 2))
 
-    level_row = lax.broadcasted_iota(jnp.int32, (nlev, cols), 0).astype(f32)
-    row_wet = ((crow[SUB - 1:SUB, :] > level_row) & (crow[SUB:SUB + 1, :] > level_row)).astype(f32)
-    row_speed = 0.5 * (ext[3, :, SUB - 1, :] + ext[3, :, SUB, :]) * row_wet
-    for q in range(4):
-        cell = [ext[q, :, SUB - 3 + i, :] for i in range(6)]
-        d = [cell[i + 1] - cell[i] for i in range(5)]
-        extra_lat[q] = face_flux(row_speed, cell[2], cell[3], *d)
-
     def beside(q, k):
         return pltpu.roll(lon_both[q], cols - 3 - wide * k, axis=1)
 
     def following(c, h):
         return left(jnp.where(lane == 0, h, c), 1)
 
-    def advect(q, k, s_lon, s_south, s_north, slot):
+    def advect_lon(q, k, s_lon):
         c = ext[q, k, SUB:top, :]
         h = beside(q, k)
         c1 = following(c, h)
@@ -304,12 +286,46 @@
             left(jnp.where(lane < 1, dh, d), 1),
             left(jnp.where(lane < 2, dh, d), 2))
         edge = pltpu.roll(extra_lon[q], cols - 2 - wide * k, axis=1)
-        along = flux - jnp.where(lane == 0, edge, right(flux, 1))
+        return flux - jnp.where(lane == 0, edge, right(flux, 1))
+
+    least_lon = jnp.minimum(count_here, following(count_here, count_beside))
+
+    def velocity_lon(i, carry):
+        for k in (2 * i, 2 * i + 1):
+            u = ext[2, k, SUB:top, :]
+            s_lon = jnp.where(least_lon > k.astype(f32), 0.5 * (u + following(u, beside(2, k))), 0.0)
+            speed_lon[k] = s_lon
+            out[2, k] = advect_lon(2, k, s_lon)
+            out[3, k] = advect_lon(3, k, s_lon)
+        return carry
+
+    lax.fori_loop(0, half, velocity_lon, 0)
+
+    level_lat.wait_recv()
+    crow[0:SUB, :] = lat_in[0, 4 * half]
+    crow[top:full, :] = lat_in[1, 4 * half]
+
+    for q in range(4):
+        for h in range(half):
+            for side, place in ((0, 0), (1, top)):
+                block = lat_in[side, q * half + h]
+                ext[q, 2 * h, place:place + SUB, :] = block
+                ext[q, 2 * h + 1, place:place + SUB, :] = pltpu.roll(block, 4, axis=0)
+
+    level_row = lax.broadcasted_iota(jnp.int32, (nlev, cols), 0).astype(f32)
+    row_wet = ((crow[SUB - 1:SUB, :] > level_row) & (crow[SUB:SUB + 1, :] > level_row)).astype(f32)
+    row_speed = 0.5 * (ext[3, :, SUB - 1, :] + ext[3, :, SUB, :]) * row_wet
+    for q in range(4):
+        cell = [ext[q, :, SUB - 3 + i, :] for i in range(6)]
+        d = [cell[i + 1] - cell[i] for i in range(5)]
+        extra_lat[q] = face_flux(row_speed, cell[2], cell[3], *d)
+
+    def advect_lat(q, k, s_south, s_north, slot):
         fbuf[slot, SUB - 1:SUB, :] = extra_lat[q, pl.ds(k, 1), :]
         fbuf[slot, SUB:2 * SUB, :] = face_rows(q, k, s_south, SUB, SUB)
         fbuf[slot, inner:top - SUB, :] = flat[q, k]
         fbuf[slot, top - SUB:top, :] = face_rows(q, k, s_north, top - SUB, SUB)
-        return along + (fbuf[slot, SUB:top, :] - fbuf[slot, SUB - 1:top - 1, :])
+        return fbuf[slot, SUB:top, :] - fbuf[slot, SUB - 1:top - 1, :]
 
     row = lax.broadcasted_iota(jnp.int32, (rows, cols), 0)
     latitude = ((y * rows + row).astype(f32) + 0.5) / float(ny * rows)
@@ -326,8 +342,6 @@
         total_beside = total_beside + jnp.where(owner >= step, right(total_beside, wide * step), 0.0)
         step *= 2
     lon_both[4] = thickness * (total_beside - 0.5 * rho_beside)
-    least_lon = jnp.minimum(count_here, following(count_here, count_beside))
-
     def momentum_level(k, slot, carry):
         above, sum_u, sum_v, star_u, star_v = carry
         level = k.astype(f32)
@@ -343,14 +357,12 @@
         grad_lat = 0.5 * (pbuf[slot, SUB + 1:top + 1, :] - pbuf[slot, SUB - 1:top - 1, :])
         u = ext[2, k, SUB:top, :]
         v = ext[3, k, SUB:top, :]
-        s_lon = jnp.where(least_lon > level, 0.5 * (u + following(u, beside(2, k))), 0.0)
         s_south = lat_speed(k, SUB, SUB)
         s_north = lat_speed(k, top - SUB, SUB)
-        speed_lon[k] = s_lon
         speed_lat[0, k] = s_south
         speed_lat[1, k] = s_north
-        accel_u = wet * (coriolis * v - advect(2, k, s_lon, s_south, s_north, 2 * slot) - grad_lon)
-        accel_v = wet * (-advect(3, k, s_lon, s_south, s_north, 2 * slot + 1) - coriolis * u - grad_lat)
+        accel_u = wet * (coriolis * v - (out[2, k] + advect_lat(2, k, s_south, s_north, 2 * slot)) - grad_lon)
+        accel_v = wet * (-(out[3, k] + advect_lat(3, k, s_south, s_north, 2 * slot + 1)) - coriolis * u - grad_lat)
         u_star = wet * u + tracer_step * accel_u
         v_star = wet * v + tracer_step * accel_v
         out[2, k] = u_star
@@ -384,7 +396,8 @@
             k = 2 * i + slot
             wet = (crow[SUB:top, :] > k.astype(f32)).astype(f32)
             for q in range(2):
-                change = advect(q, k, speed_lon[k], speed_lat[0, k], speed_lat[1, k], 2 * slot + q)
+                change = advect_lon(q, k, speed_lon[k]) + advect_lat(
+                    q, k, speed_lat[0, k], speed_lat[1, k], 2 * slot + q)
                 out[q, k] = wet * (ext[q, k, SUB:top, :] - tracer_step * change)
         return carry
 
@@ -427,15 +440,40 @@
     surf_out[0] = height[0][SUB:top]
     surf_out[1] = mean_u[0][SUB:top]
     surf_out[2] = mean_v[0][SUB:top]
-    gain[0] = zero
-    gain[1] = zero
-    gain[2] = mean_u[0][SUB:top] - mean_star_u
-    gain[3] = mean_v[0][SUB:top] - mean_star_v
+    gain[0] = mean_u[0][SUB:top] - mean_star_u
+    gain[1] = mean_v[0][SUB:top] - mean_star_v
     for part in stores:
         part.wait()
 
     for pair in (surf_lon, level_lon, level_lat, surf_lat, force_lon_pair, force_lat_pair):
         pair.wait_send()
+
+
+def finish_kernel(stars, gain, surface, counts, out, surf_out, buf, gain_buf, surf_buf, count_buf, in_sem, out_sem):
+    nlev = stars.shape[1]
+    half = nlev // 2
+    places = [(q, h) for q in (2, 3, 0, 1) for h in range(2)]
+    copy = pltpu.make_async_copy
+    small = [copy(gain, gain_buf, in_sem.at[8]), copy(counts, count_buf, in_sem.at[9]),
+             copy(surface, surf_buf, in_sem.at[10])]
+    loads = [copy(stars.at[q, h * half:(h + 1) * half], buf.at[q, h * half:(h + 1) * half], in_sem.at[i])
+             for i, (q, h) in enumerate(places)]
+    stores = [copy(buf.at[q, h * half:(h + 1) * half], out.at[q, h * half:(h + 1) * half], out_sem.at[i])
+              for i, (q, h) in enumerate(places)]
+    last = copy(surf_buf, surf_out, out_sem.at[8])
+    for part in small + loads:
+        part.start()
+    for part in small:
+        part.wait()
+    last.start()
+    for i, (q, h) in enumerate(places):
+        loads[i].wait()
+        if q >= 2:
+            for k in range(h * half, (h + 1) * half):
+                buf[q, k] = jnp.where(count_buf[...] > k, buf[q, k] + gain_buf[q - 2], 0.0)
+        stores[i].start()
+    for part in stores + [last]:
+        part.wait()
 
 
 def on_device(nx, ny, ocean_state, surface_state, column_levels):
@@ -446,7 +484,7 @@
     vmem = pltpu.VMEM
     stars, gain, surface_next = pl.pallas_call(
         functools.partial(kernel, nx, ny),
-        out_shape=(jax.ShapeDtypeStruct(ocean_state.shape, f32), jax.ShapeDtypeStruct((4, rows, cols), f32),
+        out_shape=(jax.ShapeDtypeStruct(ocean_state.shape, f32), jax.ShapeDtypeStruct((2, rows, cols), f32),
                    jax.ShapeDtypeStruct(surface_state.shape, f32)),
         in_specs=[pl.BlockSpec(memory_space=pltpu.HBM)] * 3,
         out_specs=(pl.BlockSpec(memory_space=pl.ANY), pl.BlockSpec(memory_space=vmem), pl.BlockSpec(memory_space=vmem)),
@@ -480,8 +518,21 @@
         ],
         compiler_params=pltpu.CompilerParams(collective_id=0, has_side_effects=True),
     )(ocean_state, surface_state, column_levels)
-    level = lax.broadcasted_iota(jnp.int32, stars.shape, 1)
-    return jnp.where(level < column_levels, stars + gain[:, None], 0.0), surface_next
+    parts = 8
+    return pl.pallas_call(
+        finish_kernel,
+        out_shape=(jax.ShapeDtypeStruct(ocean_state.shape, f32), jax.ShapeDtypeStruct(surface_state.shape, f32)),
+        in_specs=[pl.BlockSpec(memory_space=pl.ANY)] * 4,
+        out_specs=(pl.BlockSpec(memory_space=pl.ANY),) * 2,
+        scratch_shapes=[
+            vmem(ocean_state.shape, f32),
+            vmem((2, rows, cols), f32),
+            vmem(surface_state.shape, f32),
+            vmem((rows, cols), jnp.int32),
+            pltpu.SemaphoreType.DMA((parts + 3,)),
+            pltpu.SemaphoreType.DMA((parts + 1,)),
+        ],
+    )(stars, gain, surface_next, column_levels)
 
 
 def solution(mesh):

time: 30.8 us -> 31 us (level)
  Pallas kernels: 27 us -> 30.2 us
  other arithmetic: 2.35 us -> 0 us
  local copies, waits for them, and re-layouts: 0.63 us -> 0 us
    select_n x1 -> x0, other arithmetic: 2.35 us -> none  [on_device(): jnp.where(level < column_levels, stars + gain[:, None], 0.0)]
    pallas_call x0 -> x1, Pallas kernels: none -> 2.18 us  [on_device(): pl.pallas_call(finish_kernel, out_shape=(jax.ShapeDtypeStruct(ocean_state...]
    pallas_call x1, Pallas kernels: 27 us -> 28 us  [on_device(): pl.pallas_call(functools.partial(kernel, nx, ny), out_shape=(jax.ShapeDty...]
    unnamed x5 -> x0, local copies, waits for them, and re-layouts: 0.63 us -> none
where the time goes in v5:
time: 31 us; the launch traced here: 30.8 us
  Pallas kernels  30.2 us (97%)
  between operations  0.64 us (2%)
    pallas_call x1, Pallas kernels, on_device(): pl.pallas_call(functools.partial(kernel, nx, ny), out_shape=(jax.ShapeDty...  28 us
    pallas_call x1, Pallas kernels, on_device(): pl.pallas_call(finish_kernel, out_shape=(jax.ShapeDtypeStruct(ocean_state...  2.18 us

profile of v5, /device:TPU:1, one launch (start us, length us, event | category | flops | bytes accessed | tf_op | source)
XLA Modules:
  0.0 30.8 jit_solution(3629666807470359160)
XLA Ops:
  0.6 28.0 %shard_map.50 = (f32[4,16,32,128]{3,2,1,0:T(8,128)}, f32[2,32,128]{2,1,0:T(8,128)}, f32[3,32,128]{2,1,0:T(8,128)}) custom-call(f32[4,16,32,128]{3,2,1,0:T(8,128)} %ocean.1, f32[3,32,128]{2,1,0:T(8,128)} %surface.1, s32[32,128]{1,0:T(8,128)} %counts.1), custom_call_target="tpu_custom_call" | custom-call | tf_op jit(solution)/shard_map/pallas_call | solution.py:485
  28.6 2.2 %shard_map.51 = (f32[4,16,32,128]{3,2,1,0:T(8,128)}, f32[3,32,128]{2,1,0:T(8,128)}) custom-call(f32[4,16,32,128]{3,2,1,0:T(8,128)} %get-tuple-element.5.stars, f32[2,32,128]{2,1,0:T(8,128)} %get-tuple-element.6.gain, f32[3,32,128]{2,1,0:T(8,128)} %get-tuple-element.7.surface, s32[32,128]{1,0:T(8,128)} %counts.1), custom_call_target="tpu_custom_call" | custom-call | tf_op jit(solution)/shard_map/pallas_call | solution.py:522

commit v6 on v5

--- a/solution.py
+++ b/solution.py
@@ -54,7 +54,7 @@
 
 
 def kernel(nx, ny, ocean, surface, levels_in, out_hbm, gain, surf_out, ext, lon_own, lon_in, lat_out, lat_in, sa, sf,
-           sa_lon, sf_lon, sa_north, sf_north, extra_lon, extra_lat, speed_lon, speed_lat, pbuf, fbuf,
+           sa_lon, sf_lon, sa_north, sf_north, extra_lon, extra_lat, speed_lon, pbuf, fbuf,
            flat, out, counts, crow, lon_both, local_sem, store_sem, send_sem, recv_sem):
     nlev, rows, cols = ocean.shape[1], ocean.shape[2], ocean.shape[3]
     top = SUB + rows
@@ -236,8 +236,8 @@
     def inner_faces(i, carry):
         for k in (2 * i, 2 * i + 1):
             s = lat_speed(k, inner, inner_count)
-            for q in range(4):
-                flat[q, k] = face_rows(q, k, s, inner, inner_count)
+            for q in (2, 3):
+                flat[q - 2, k] = face_rows(q, k, s, inner, inner_count)
         return carry
 
     lax.fori_loop(0, half, inner_faces, 0)
@@ -290,17 +290,6 @@
 
     least_lon = jnp.minimum(count_here, following(count_here, count_beside))
 
-    def velocity_lon(i, carry):
-        for k in (2 * i, 2 * i + 1):
-            u = ext[2, k, SUB:top, :]
-            s_lon = jnp.where(least_lon > k.astype(f32), 0.5 * (u + following(u, beside(2, k))), 0.0)
-            speed_lon[k] = s_lon
-            out[2, k] = advect_lon(2, k, s_lon)
-            out[3, k] = advect_lon(3, k, s_lon)
-        return carry
-
-    lax.fori_loop(0, half, velocity_lon, 0)
-
     level_lat.wait_recv()
     crow[0:SUB, :] = lat_in[0, 4 * half]
     crow[top:full, :] = lat_in[1, 4 * half]
@@ -323,7 +312,7 @@
     def advect_lat(q, k, s_south, s_north, slot):
         fbuf[slot, SUB - 1:SUB, :] = extra_lat[q, pl.ds(k, 1), :]
         fbuf[slot, SUB:2 * SUB, :] = face_rows(q, k, s_south, SUB, SUB)
-        fbuf[slot, inner:top - SUB, :] = flat[q, k]
+        fbuf[slot, inner:top - SUB, :] = flat[q - 2, k]
         fbuf[slot, top - SUB:top, :] = face_rows(q, k, s_north, top - SUB, SUB)
         return fbuf[slot, SUB:top, :] - fbuf[slot, SUB - 1:top - 1, :]
 
@@ -357,12 +346,12 @@
         grad_lat = 0.5 * (pbuf[slot, SUB + 1:top + 1, :] - pbuf[slot, SUB - 1:top - 1, :])
         u = ext[2, k, SUB:top, :]
         v = ext[3, k, SUB:top, :]
+        s_lon = jnp.where(least_lon > level, 0.5 * (u + following(u, beside(2, k))), 0.0)
+        speed_lon[k] = s_lon
         s_south = lat_speed(k, SUB, SUB)
         s_north = lat_speed(k, top - SUB, SUB)
-        speed_lat[0, k] = s_south
-        speed_lat[1, k] = s_north
-        accel_u = wet * (coriolis * v - (out[2, k] + advect_lat(2, k, s_south, s_north, 2 * slot)) - grad_lon)
-        accel_v = wet * (-(out[3, k] + advect_lat(3, k, s_south, s_north, 2 * slot + 1)) - coriolis * u - grad_lat)
+        accel_u = wet * (coriolis * v - (advect_lon(2, k, s_lon) + advect_lat(2, k, s_south, s_north, 2 * slot)) - grad_lon)
+        accel_v = wet * (-(advect_lon(3, k, s_lon) + advect_lat(3, k, s_south, s_north, 2 * slot + 1)) - coriolis * u - grad_lat)
         u_star = wet * u + tracer_step * accel_u
         v_star = wet * v + tracer_step * accel_v
         out[2, k] = u_star
@@ -395,13 +384,17 @@
         for slot in range(2):
             k = 2 * i + slot
             wet = (crow[SUB:top, :] > k.astype(f32)).astype(f32)
+            s_lat = lat_speed(k, SUB, rows)
             for q in range(2):
-                change = advect_lon(q, k, speed_lon[k]) + advect_lat(
-                    q, k, speed_lat[0, k], speed_lat[1, k], 2 * slot + q)
+                flux = face_rows(q, k, s_lat, SUB, rows)
+                place = 2 * slot + q
+                fbuf[place, SUB - 1:SUB, :] = extra_lat[q, pl.ds(k, 1), :]
+                fbuf[place, SUB:top, :] = flux
+                change = advect_lon(q, k, speed_lon[k]) + (flux - fbuf[place, SUB - 1:top - 1, :])
                 out[q, k] = wet * (ext[q, k, SUB:top, :] - tracer_step * change)
         return carry
 
-    mid = half // 2
+    mid = (3 * half) // 8
     lax.fori_loop(0, mid, tracers, 0)
     force_lon_pair.wait_recv()
     close_lon(sf, sf_lon, 2)
@@ -503,10 +496,9 @@
             vmem((4, rows, cols), f32),
             vmem((4, nlev, cols), f32),
             vmem((nlev, rows, cols), f32),
-            vmem((2, nlev, SUB, cols), f32),
             vmem((2, full, cols), f32),
             vmem((4, full, cols), f32),
-            vmem((4, nlev, rows - 2 * SUB, cols), f32),
+            vmem((2, nlev, rows - 2 * SUB, cols), f32),
             vmem((4, nlev, rows, cols), f32),
             vmem((rows, cols), jnp.int32),
             vmem((full, cols), f32),

time: 31 us -> 30.1 us (0.971)
  Pallas kernels: 30.2 us -> 29.3 us
    pallas_call x1, Pallas kernels: 28 us -> 27.1 us  [on_device(): pl.pallas_call(functools.partial(kernel, nx, ny), out_shape=(jax.ShapeDty...]
where the time goes in v6:
time: 30.1 us; the launch traced here: 30 us
  Pallas kernels  29.3 us (97%)
  between operations  0.64 us (2%)
    pallas_call x1, Pallas kernels, on_device(): pl.pallas_call(functools.partial(kernel, nx, ny), out_shape=(jax.ShapeDty...  27.1 us
    pallas_call x1, Pallas kernels, on_device(): pl.pallas_call(finish_kernel, out_shape=(jax.ShapeDtypeStruct(ocean_state...  2.18 us

profile of v6, /device:TPU:1, one launch (start us, length us, event | category | flops | bytes accessed | tf_op | source)
XLA Modules:
  0.0 30.0 jit_solution(14960545678455940396)
XLA Ops:
  0.6 27.1 %shard_map.50 = (f32[4,16,32,128]{3,2,1,0:T(8,128)}, f32[2,32,128]{2,1,0:T(8,128)}, f32[3,32,128]{2,1,0:T(8,128)}) custom-call(f32[4,16,32,128]{3,2,1,0:T(8,128)} %ocean.1, f32[3,32,128]{2,1,0:T(8,128)} %surface.1, s32[32,128]{1,0:T(8,128)} %counts.1), custom_call_target="tpu_custom_call" | custom-call | tf_op jit(solution)/shard_map/pallas_call | solution.py:478
  27.8 2.2 %shard_map.51 = (f32[4,16,32,128]{3,2,1,0:T(8,128)}, f32[3,32,128]{2,1,0:T(8,128)}) custom-call(f32[4,16,32,128]{3,2,1,0:T(8,128)} %get-tuple-element.5.stars, f32[2,32,128]{2,1,0:T(8,128)} %get-tuple-element.6.gain, f32[3,32,128]{2,1,0:T(8,128)} %get-tuple-element.7.surface, s32[32,128]{1,0:T(8,128)} %counts.1), custom_call_target="tpu_custom_call" | custom-call | tf_op jit(solution)/shard_map/pallas_call | solution.py:514

commit v7 on v6

--- a/solution.py
+++ b/solution.py
@@ -156,17 +156,17 @@
     owner = lane // wide
     sub8 = lax.broadcasted_iota(jnp.int32, (SUB, cols), 0)
 
-    def mirrored(block):
-        for axis, length in ((0, SUB), (1, cols)):
-            at = lax.broadcasted_iota(jnp.int32, block.shape, axis)
-            size = block.shape[axis]
+    def mirrored(tiles):
+        for axis, length in ((1, SUB), (2, cols)):
+            at = lax.broadcasted_iota(jnp.int32, tiles.shape, axis)
             step = 1
             while step < length:
-                up = pltpu.roll(block, step, axis=axis)
-                down = pltpu.roll(block, size - step, axis=axis)
-                block = jnp.where((at // step) % 2 == 1, up, down)
+                turned = pltpu.roll(tiles, step, axis=axis)
+                if 2 * step < length:
+                    turned = jnp.where((at // step) % 2 == 1, turned, pltpu.roll(tiles, length - step, axis=axis))
+                tiles = turned
                 step *= 2
-        return block
+        return tiles
 
     load.wait()
     half = nlev // 2
@@ -188,11 +188,8 @@
 
     @pl.when(at_north)
     def _():
-        lat_out[0, 4 * half] = mirrored(lat_out[0, 4 * half])
-        for q in range(4):
-            sign = 1.0 if q < 2 else -1.0
-            block = lat_out[0, q * half:(q + 1) * half].reshape(half * SUB, cols)
-            lat_out[0, q * half:(q + 1) * half] = (sign * mirrored(block)).reshape(half, SUB, cols)
+        lat_out[0] = mirrored(jnp.concatenate(
+            [lat_out[0, 0:2 * half], -lat_out[0, 2 * half:4 * half], lat_out[0, 4 * half:]], axis=0))
 
     pl.semaphore_wait(barrier, 3 + jnp.where(y > 0, 1, 0))
     level_lat.start()
@@ -217,9 +214,8 @@
 
         @pl.when(at_north)
         def _():
-            for f in range(count):
-                block = staged[f].reshape(2 * SUB, cols)
-                staged[f] = (signs[f] * mirrored(block)).reshape(2, SUB, cols)
+            staged[...] = mirrored(jnp.concatenate(
+                [signs[f] * staged[f] for f in range(count)], axis=0)).reshape(count, 2, SUB, cols)
 
     def face_rows(q, k, s, first, count):
         start = first - 2 + jnp.minimum(k, 0)
@@ -404,7 +400,6 @@
     lax.fori_loop(mid, half, tracers, 0)
     stores.append(store(0, 2 * mid, nlev, 2))
     surf_lat.wait_recv()
-    force_lat_pair.wait_recv()
 
     def slope_lon(c, h):
         up_c = left(jnp.where(lane_full == 0, h, c), 1)
@@ -422,12 +417,14 @@
     mean_v = [sa[2, i] for i in both]
     depth = [thickness * sa[3, i] for i in both]
     sea = [(sa[3, i] > 0.0).astype(f32) for i in both]
-    for _ in range(NSUB):
+    for substep in range(NSUB):
         dx = slope_lon(*[depth[i] * mean_u[i] for i in both])
         dy = slope_lat(*[depth[i] * mean_v[i] for i in both])
         height = [sea[i] * (height[i] - surface_step * (dx[i] + dy[i])) for i in both]
         dx = slope_lon(*height)
         dy = slope_lat(*height)
+        if substep == 0:
+            force_lat_pair.wait_recv()
         mean_u = [sea[i] * (mean_u[i] + surface_step * (sf[0, i] - dx[i])) for i in both]
         mean_v = [sea[i] * (mean_v[i] + surface_step * (sf[1, i] - dy[i])) for i in both]
     surf_out[0] = height[0][SUB:top]

time: 30.1 us -> 29.8 us (0.990)
  no operation moved by 1% of the time
where the time goes in v7:
time: 29.8 us; the launch traced here: 29.7 us
  Pallas kernels  29 us (97%)
  between operations  0.64 us (2%)
    pallas_call x1, Pallas kernels, on_device(): pl.pallas_call(functools.partial(kernel, nx, ny), out_shape=(jax.ShapeDty...  26.9 us
    pallas_call x1, Pallas kernels, on_device(): pl.pallas_call(finish_kernel, out_shape=(jax.ShapeDtypeStruct(ocean_state...  2.18 us

profile of v7, /device:TPU:1, one launch (start us, length us, event | category | flops | bytes accessed | tf_op | source)
XLA Modules:
  0.0 29.7 jit_solution(2476092131651121054)
XLA Ops:
  0.6 26.9 %shard_map.50 = (f32[4,16,32,128]{3,2,1,0:T(8,128)}, f32[2,32,128]{2,1,0:T(8,128)}, f32[3,32,128]{2,1,0:T(8,128)}) custom-call(f32[4,16,32,128]{3,2,1,0:T(8,128)} %ocean.1, f32[3,32,128]{2,1,0:T(8,128)} %surface.1, s32[32,128]{1,0:T(8,128)} %counts.1), custom_call_target="tpu_custom_call" | custom-call | tf_op jit(solution)/shard_map/pallas_call | solution.py:475
  27.5 2.2 %shard_map.51 = (f32[4,16,32,128]{3,2,1,0:T(8,128)}, f32[3,32,128]{2,1,0:T(8,128)}) custom-call(f32[4,16,32,128]{3,2,1,0:T(8,128)} %get-tuple-element.5.stars, f32[2,32,128]{2,1,0:T(8,128)} %get-tuple-element.6.gain, f32[3,32,128]{2,1,0:T(8,128)} %get-tuple-element.7.surface, s32[32,128]{1,0:T(8,128)} %counts.1), custom_call_target="tpu_custom_call" | custom-call | tf_op jit(solution)/shard_map/pallas_call | solution.py:511
